TPU v7x, 768 devices: a whole 4x8x12 slice. The times are simulated.
768 devices in a mesh: term: 64 (over x, y, core), sector: 12 (over z).
Axes of the slice: x: 4, y: 8, z: 12, core: 2. Of those that a mesh axis runs over, the one named last changes fastest.
Arguments:
- psi: bfloat16 [12, 512, 512], P('sector', 'term'), may hold values from -6 to 6
- sizes: int32 [12], P('sector'), may hold values from 128 to 512, as said below
- left_ops: bfloat16 [256, 12, 512, 512], P('term', 'sector'), may hold values from -0.015625 to 0.015625
- right_ops: bfloat16 [256, 12, 512, 512], P('term', 'sector'), may hold values from -0.25 to 0.25
- source: int32 [256, 12], P('term', 'sector'), may hold values from 0 to 11
Outputs:
- sigma: bfloat16 [512, 12, 512], P('term', 'sector')
Inputs may be any that keep to these rules, and one draw needn't show every extreme that they name: `sizes`: each is a multiple of 128; some sector has the full 512.
All inputs are finite; a program needn't handle non-finite values.
Results may differ from a plain program's by a relative error of at most 0.0049.
Values may be sent and summed in bfloat16 or wider, within the bound.
No kernel may reach another device: no remote copies, remote signals or barrier semaphores. Data moves between devices by JAX's collectives and lax.ppermute only.
A program may use at most 32 MiB of HBM per device.

v0:
```python
import jax
import jax.numpy as jnp
from jax import lax
from jax.sharding import PartitionSpec as P


def on_device(psi, sizes, left_ops, right_ops, source):
    term_count = left_ops.shape[0]
    sector_count = left_ops.shape[1]
    block_size = left_ops.shape[2]
    pair_count = term_count * sector_count
    row_share = psi.shape[1]
    wanted = source.reshape(pair_count)
    rows_all, sizes_all = (
        lax.all_gather(psi, "sector", axis=0, tiled=True),
        lax.all_gather(sizes, "sector", axis=0, tiled=True),
    )
    picked = lax.all_gather(rows_all, "term", axis=1, tiled=True)[wanted]
    picked_size = sizes_all[wanted]
    positions = jnp.arange(block_size, dtype=jnp.int32)
    inside = (positions[None, :, None] < picked_size[:, None, None]) & (
        positions[None, None, :] < picked_size[:, None, None]
    )
    masked = jnp.where(inside, picked, jnp.zeros((), jnp.bfloat16))
    right_flat = right_ops.reshape(pair_count, block_size, block_size)
    product = jnp.einsum(
        "pab,pbc->pac", masked, right_flat, preferred_element_type=jnp.float32
    ).astype(jnp.bfloat16)
    product = product.reshape(term_count, sector_count, block_size, block_size)
    row_first = lax.axis_index("term") * row_share
    complete = lax.psum(
        jnp.einsum("ksab,ksbc->asc", left_ops, product, preferred_element_type=jnp.float32), "term"
    )
    summed = lax.dynamic_slice_in_dim(complete, row_first, row_share, 0)
    global_rows = row_first + jnp.arange(row_share, dtype=jnp.int32)
    keep = (global_rows[:, None, None] < sizes[None, :, None]) & (
        positions[None, None, :] < sizes[None, :, None]
    )
    return jnp.where(keep, summed, jnp.float32(0.0)).astype(jnp.bfloat16)


def solution(mesh):
    return jax.shard_map(
        on_device,
        mesh=mesh,
        in_specs=(
            P("sector", "term", None),
            P("sector"),
            P("term", "sector", None, None),
            P("term", "sector", None, None),
            P("term", "sector"),
        ),
        out_specs=P("term", "sector", None),
        check_vma=False,
    )
```

profile of v0, /device:TPU:64, one launch (start us, length us, event | category | flops | bytes accessed | tf_op | source)
XLA Modules:
  0.0 405.7 jit_solution(15819924574189838988)
XLA Ops:
  6.5 0.0 copy-start
  6.5 0.0 all-gather.2.cloned.1.call-start
  6.5 31.8 %all_gather.10 = bf16[12,8,512]{2,1,0:T(8,128)(2,1)} all-gather(bf16[1,8,512]{2,1,0:T(8,128)(2,1)} %param.5), channel_id=1, replica_groups=mesh['term'=64,'sector'=12] {'sector'}, dimensions={0}, use_global_device_ids=true | all-gather | bytes 106496 | tf_op jit(solution)/shard_map/all_gather | solution.py:15
  38.3 0.0 all-gather.2.cloned.1.call-update
  39.0 1.3 dynamic-slice
  40.4 0.7 dynamic-update-slice
  41.1 23.2 %all-reduce = s32[12]{0:T(128)S(1)} all-reduce(s32[12]{0:T(128)S(1)} %dynamic-update-slice), channel_id=1, replica_groups=mesh['term'=64,'sector'=12] {'sector'}, use_global_device_ids=true, to_apply=%add | all-reduce | flops 12 | bytes 96
  64.3 0.7 fusion.18
  65.0 0.6 gather_fusion
  65.7 0.1 iota_compare_fusion
  65.7 61.0 %all-gather.2.cloned.1.call-done = bf16[12,512,512]{2,1,0:T(8,128)(2,1)} async-done(((bf16[12,8,512]{2,1,0:T(8,128)(2,1)}), bf16[12,512,512]{2,1,0:T(8,128)(2,1)}) %all-gather.2.cloned.1.call-update) | async-done | bytes 6291472 | tf_op jit(solution)/shard_map/all_gather | solution.py:18
  126.7 4.8 %gather_fusion.1 = bf16[4,512,512]{2,1,0:T(8,128)(2,1)} fusion(bf16[12,512,512]{2,1,0:T(8,128)(2,1)} %all-gather.2.cloned.1.call-done, s32[1024]{0:T(1024)S(1)} %pad_clamp_fusion), kind=kCustom, calls=%fused_computation.1 | custom fusion | bytes 4194320 | tf_op jit(solution)/shard_map/gather | solution.py:18
  131.5 0.0 copy-done
  131.5 4.6 %fusion.7 = f32[512,1,512]{2,0,1:T(8,128)S(1)} fusion(bf16[4,1,512,512]{3,2,1,0:T(8,128)(2,1)S(1)} %copy-done, bf16[4,512,512]{2,1,0:T(8,128)(2,1)} %gather_fusion.1, bf16[4,1,512,512]{3,2,1,0:T(8,128)(2,1)} %param.8, pred[4,512]{1,0:T(4,128)(4,1)S(1)} %iota_compare_fusion), kind=kOutput, calls=%fused_computation.10 | convolution fusion | flops 2150629376 | bytes 7342080 | tf_op jit(solution)/shard_map/ksab,ksbc->asc/dot_general | solution.py:32
  136.1 261.3 %all-reduce.2 = bf16[512,1,512]{2,0,1:T(8,128)(2,1)} all-reduce(f32[512,1,512]{2,0,1:T(8,128)S(1)} %fusion.7), channel_id=1, replica_groups=mesh['term'=64,'sector'=12] {'term'}, use_global_device_ids=true, to_apply=%region_0.1 | all-reduce | flops 262144 | bytes 1572864 | tf_op jit(solution)/shard_map/psum | solution.py:31
  397.5 1.4 select_convert_fusion
  (4 shorter events, 0.0 us)
Async XLA Ops:
  6.5 125.0 %copy-start = (bf16[4,1,512,512]{3,2,1,0:T(8,128)(2,1)S(1)}, bf16[4,1,512,512]{3,2,1,0:T(8,128)(2,1)}, u32[]{:S(2)}) copy-start(bf16[4,1,512,512]{3,2,1,0:T(8,128)(2,1)} %param.7) | copy-start | bytes 6291460
  6.5 120.2 %all-gather.2.cloned.1.call-start = ((), (), s32[]{:S(2)}) async-start(), calls=%async_computation | async-start | bytes 6389760 | tf_op jit(solution)/shard_map/all_gather | solution.py:18
Sparse Core Ops, SparseCore 0:
  38.5 88.1 all-gather.1
where the time goes:
time: 406 us
  blocking collectives  316 us (78%)
  waiting for transfers between devices  61 us (15%)
  between operations  14.1 us (3%)
  local copies, waits for them, and re-layouts  7.51 us (2%)
  matrix products  4.6 us (1%)
    psum x1, blocking collectives, on_device(): lax.psum(jnp.einsum('ksab,ksbc->asc', left_ops, product, preferred_elemen...  261 us
    all_gather x1, waiting for transfers between devices, on_device(): picked = lax.all_gather(rows_all, 'term', axis=1, tiled=True)[wanted]  61 us
    all_gather x1, blocking collectives, on_device(): lax.all_gather(psi, 'sector', axis=0, tiled=True)  31.8 us
    unnamed x1, blocking collectives  23.2 us
  transfers between devices with their start and end apart: 1, of which 1 were waited for; matrix products, arithmetic and copies ran while one was open for 1% of the time, Pallas kernels for 0%

commit v1 on v0

v1 whole, which is shorter than its diff:
```python
import functools

import jax
import jax.numpy as jnp
from jax import lax
from jax.experimental import pallas as pl
from jax.experimental.pallas import tpu as pltpu
from jax.sharding import Mesh
from jax.sharding import PartitionSpec as P

NX, NY, NC, NZ = 4, 8, 2, 12
B = 512
ROWS = 8
HALF = B // 2
PART = HALF // NX
ORDER = (0, 2, 4, 6, 1, 3, 5, 7)
CHIP = ("x", "y")
ALL = ("x", "y", "c", "z")


def diagonal_groups():
    return [[((a - z) % NX) * NZ + z for z in range(NZ)] for a in range(NX)]


def plane_groups():
    return [[((h - 2 * y) % NX) * NY + y for y in ORDER] for h in range(NX)]


def shifts(core0, core1):
    pairs = []
    for x in range(NX):
        for y in range(NY):
            for c in range(NC):
                for z in range(NZ):
                    dx, dy, dz = core0 if c == 0 else core1
                    at = ((x * NY + y) * NC + c) * NZ + z
                    come = (((x + dx) % NX * NY + (y + dy) % NY) * NC + c) * NZ + (z + dz) % NZ
                    pairs.append((come, at))
    return pairs


def split_columns(core_ref, left_ref, own_ref, other_ref):
    core = core_ref[0]
    row = lax.broadcasted_iota(jnp.int32, (B, B), 0)
    col = lax.broadcasted_iota(jnp.int32, (B, B), 1)
    where_from = (
        ((col >> 6) & 3) * 128
        + ((col >> 3) & 3) * 32
        + ((col >> 5) & 1) * 16
        + (((col >> 8) & 1) ^ core) * 8
        + (col & 7)
    )
    pick = jnp.where(row == where_from, 1.0, 0.0).astype(jnp.bfloat16)
    moved = jnp.dot(left_ref[0], pick, preferred_element_type=jnp.float32).astype(jnp.bfloat16)
    own_ref[0] = moved[:, :HALF]
    other_ref[0] = moved[:, HALF:]


def matvec(
    wanted_ref,
    at_ref,
    a0,
    a1,
    a2,
    a3,
    b0,
    b1,
    b2,
    b3,
    right_a,
    right_b,
    left_a,
    left_b,
    keep_ref,
    send_ref,
    total,
    product_a,
    product_b,
):
    step = pl.program_id(0)

    def one(parts, right, left, product, slot):
        start = at_ref[0] + 16 - wanted_ref[slot]
        rows = jnp.concatenate([p[...].reshape(PART, B) for p in parts], axis=0)
        result = jnp.dot(rows, right[0], preferred_element_type=jnp.float32).astype(jnp.bfloat16)
        for q in range(4):
            for odd in range(2):
                piece = result[q * PART + odd * 32 : q * PART + odd * 32 + 32]
                product[(start + q - 2 * odd) & 3, odd] = piece
        return jnp.dot(
            left[0], product[...].reshape(HALF, B), preferred_element_type=jnp.float32
        )

    both = one((a0, a1, a2, a3), right_a, left_a, product_a, step) + one(
        (b0, b1, b2, b3), right_b, left_b, product_b, step + 4
    )

    @pl.when(step == 0)
    def _():
        total[...] = both

    @pl.when(step > 0)
    def _():
        total[...] += both

    @pl.when(step == pl.num_programs(0) - 1)
    def _():
        pairs = total[...].reshape(NX * NY, 2, ROWS, B)
        low, high = pairs[:, 0], pairs[:, 1]
        first = at_ref[1] == 0
        keep_ref[...] = jnp.where(first, low, high)
        send_ref[...] = jnp.where(first, high, low).astype(jnp.bfloat16)


def on_device(psi, sizes, left_ops, right_ops, source):
    x, y, c, z = (lax.axis_index(a) for a in ALL)
    term_count = left_ops.shape[0]
    swap = [(0, 1), (1, 0)]
    left = left_ops.reshape(term_count, B, B)
    right = right_ops.reshape(term_count, B, B)
    wanted = source.reshape(term_count)

    own_rows = ((x * NY + y) * NC + c) * ROWS + jnp.arange(ROWS, dtype=jnp.int32)
    columns = jnp.arange(B, dtype=jnp.int32)
    inside = (own_rows[:, None] < sizes[0]) & (columns[None, :] < sizes[0])
    masked = jnp.where(inside, psi[0], jnp.zeros((), psi.dtype))

    core = c.astype(jnp.int32).reshape(1)
    left_own, left_other = pl.pallas_call(
        split_columns,
        grid_spec=pltpu.PrefetchScalarGridSpec(
            num_scalar_prefetch=1,
            grid=(term_count,),
            in_specs=[pl.BlockSpec((1, B, B), lambda k, core: (k, 0, 0))],
            out_specs=[pl.BlockSpec((1, B, HALF), lambda k, core: (k, 0, 0))] * 2,
        ),
        out_shape=[jax.ShapeDtypeStruct((term_count, B, HALF), jnp.bfloat16)] * 2,
        cost_estimate=pl.CostEstimate(flops=2 * term_count * B**3, bytes_accessed=4 * term_count * B * B, transcendentals=0),
    )(core, left)
    right_far = lax.ppermute(right, "c", swap)
    left_far = lax.ppermute(left_other, "c", swap)
    wanted_far = lax.ppermute(wanted, "c", swap)

    by_sector = lax.all_to_all(
        jnp.broadcast_to(masked[None], (NZ, ROWS, B)),
        ("x", "z"),
        0,
        0,
        axis_index_groups=diagonal_groups(),
        tiled=True,
    )
    part = lax.all_to_all(
        jnp.broadcast_to(by_sector[None], (NY, NZ, ROWS, B)),
        CHIP,
        0,
        0,
        axis_index_groups=plane_groups(),
        tiled=True,
    )
    part = part.transpose(1, 0, 2, 3).reshape(NZ, PART, B)
    up = lax.ppermute(part, ALL, shifts((1, 0, 0), (0, 0, 1)))
    down = lax.ppermute(part, ALL, shifts((-1, 0, 0), (0, 0, -1)))
    across = lax.ppermute(part, ALL, shifts((0, 1, 0), (0, -1, 0)))
    parts = (part, up, across, down)

    near = [pl.BlockSpec((1, PART, B), lambda k, w, at: (w[k], 0, 0))] * 4
    far = [pl.BlockSpec((1, PART, B), lambda k, w, at: (w[k + 4], 0, 0))] * 4
    whole = pl.BlockSpec((1, B, B), lambda k, w, at: (k, 0, 0))
    halved = pl.BlockSpec((1, B, HALF), lambda k, w, at: (k, 0, 0))
    result = pl.BlockSpec((NX * NY, ROWS, B), lambda k, w, at: (0, 0, 0))
    keep, send = pl.pallas_call(
        matvec,
        grid_spec=pltpu.PrefetchScalarGridSpec(
            num_scalar_prefetch=2,
            grid=(term_count,),
            in_specs=near + far + [whole, whole, halved, halved],
            out_specs=[result, result],
            scratch_shapes=[
                pltpu.VMEM((B, B), jnp.float32),
                pltpu.VMEM((4, 2, 32, B), jnp.bfloat16),
                pltpu.VMEM((4, 2, 32, B), jnp.bfloat16),
            ],
        ),
        out_shape=[
            jax.ShapeDtypeStruct((NX * NY, ROWS, B), jnp.float32),
            jax.ShapeDtypeStruct((NX * NY, ROWS, B), jnp.bfloat16),
        ],
        compiler_params=pltpu.CompilerParams(vmem_limit_bytes=32 * 1024 * 1024),
        cost_estimate=pl.CostEstimate(flops=8 * term_count * HALF * B * B, bytes_accessed=16 * term_count * HALF * B, transcendentals=0),
    )(
        jnp.concatenate([wanted, wanted_far]),
        jnp.stack([(x + 2 * y + z).astype(jnp.int32), c.astype(jnp.int32)]),
        *parts,
        *parts,
        right,
        right_far,
        left_own,
        left_far,
    )
    chip_sum = keep + lax.ppermute(send, "c", swap).astype(jnp.float32)
    shares = lax.all_to_all(chip_sum.astype(jnp.bfloat16), CHIP, 0, 0, tiled=True)
    summed = jnp.sum(shares.astype(jnp.float32), axis=0)
    return jnp.where(inside, summed, jnp.float32(0.0)).astype(jnp.bfloat16)[:, None, :]


def solution(mesh):
    fine = Mesh(mesh.devices.reshape(NX, NY, NC, NZ), ALL)
    term = ("x", "y", "c")
    return jax.shard_map(
        on_device,
        mesh=fine,
        in_specs=(
            P("z", term, None),
            P("z"),
            P(term, "z", None, None),
            P(term, "z", None, None),
            P(term, "z"),
        ),
        out_specs=P(term, "z", None),
        check_vma=False,
    )
```

time: 406 us -> 115 us (0.28)
  the two profiles are of different devices: /device:TPU:64 before, /device:TPU:8 now
where the time goes in v1:
time: 115 us; the launch traced here: 114 us
  blocking collectives  51 us (44%)
  starting transfers between devices  26.3 us (23%)
  waiting for transfers between devices  21 us (18%)
  Pallas kernels  10.8 us (9%)
  local copies, waits for them, and re-layouts  2.29 us (2%)
  other arithmetic  1.74 us (2%)
    all_to_all x1, blocking collectives, on_device(): lax.all_to_all(jnp.broadcast_to(masked[None], (NZ, ROWS, B)), ('x', 'z'),...  30.5 us
    all_to_all x1, blocking collectives, on_device(): lax.all_to_all(chip_sum.astype(jnp.bfloat16), CHIP, 0, 0, tiled=True)  20.5 us
    all_to_all x1, waiting for transfers between devices, on_device(): lax.all_to_all(jnp.broadcast_to(by_sector[None], (NY, NZ, ROWS, B)), CHIP...  9.39 us
    all_to_all x1, starting transfers between devices, on_device(): lax.all_to_all(jnp.broadcast_to(by_sector[None], (NY, NZ, ROWS, B)), CHIP...  9.17 us
    pallas_call x1, Pallas kernels, on_device(): pl.pallas_call(matvec, grid_spec=pltpu.PrefetchScalarGridSpec(num_scalar_...  6.14 us
    ppermute x1, waiting for transfers between devices, on_device(): down = lax.ppermute(part, ALL, shifts((-1, 0, 0), (0, 0, -1)))  5.88 us
    pallas_call x1, Pallas kernels, on_device(): pl.pallas_call(split_columns, grid_spec=pltpu.PrefetchScalarGridSpec(num_...  4.62 us
    ppermute x1, starting transfers between devices, on_device(): up = lax.ppermute(part, ALL, shifts((1, 0, 0), (0, 0, 1)))  3.6 us
  transfers between devices with their start and end apart: 8, of which 5 were waited for; matrix products, arithmetic and copies ran while one was open for 0% of the time, Pallas kernels for 4%

profile of v1, /device:TPU:8, one launch (start us, length us, event | category | flops | bytes accessed | tf_op | source)
XLA Modules:
  0.0 113.9 jit_solution(8338785467572710331)
XLA Ops:
  0.0 0.0 copy-start.1
  0.7 0.8 fusion.1
  1.5 30.5 %all_to_all.15 = bf16[12,8,512]{2,1,0:T(8,128)(2,1)S(1)} all-to-all(bf16[12,8,512]{2,1,0:T(8,128)(2,1)S(1)} %broadcast_in_dim.27), channel_id=1, replica_groups={{0,577,386,195,4,581,390,199,8,585,394,203},{192,1,578,387,196,5,582,39..., dimensions={0} | all-to-all | bytes 196608 | tf_op jit(solution)/shard_map/all_to_all | solution.py:144
  31.9 1.0 broadcast_in_dim.28
  32.9 9.2 %all-to-all-start.1 = ((bf16[8,12,8,512]{3,2,1,0:T(8,128)(2,1)}), bf16[8,12,8,512]{3,2,1,0:T(8,128)(2,1)S(1)}, u32[]{:S(2)}, u32[]{:S(2)}) async-start(bf16[8,12,8,512]{3,2,1,0:T(8,128)(2,1)} %broadcast_in_dim.28), calls=%async_computation.1 | async-start | bytes 1572864 | tf_op jit(solution)/shard_map/all_to_all | solution.py:152
  42.1 1.9 %collective-permute-start.4 = (bf16[4,512,512]{2,1,0:T(8,128)(2,1)}, bf16[4,512,512]{2,1,0:T(8,128)(2,1)}, u32[]{:S(2)}, u32[]{:S(2)}) collective-permute-start(bf16[4,512,512]{2,1,0:T(8,128)(2,1)} %bitcast.7.right_a), channel_id=1, source_target_pairs={{0,12},{12,0},{1,13},{13,1},{2,14},{14,2},{3,15},{15,3},{4,16},{16... | collective-permute-start | bytes 6291464 | tf_op jit(solution)/shard_map/ppermute | solution.py:140
  44.0 0.0 copy-done.1
  44.0 2.4 %collective-permute-start = (s32[4]{0:T(128)S(1)}, s32[4]{0:T(128)S(1)}, u32[]{:S(2)}, u32[]{:S(2)}) collective-permute-start(s32[4]{0:T(128)S(1)} %bitcast.20), channel_id=1, source_target_pairs={{0,12},{12,0},{1,13},{13,1},{2,14},{14,2},{3,15},{15,3},{4,16},{16... | collective-permute-start | bytes 56 | tf_op jit(solution)/shard_map/ppermute | solution.py:142
  46.4 4.6 %shard_map.55 = (bf16[4,512,256]{2,1,0:T(8,128)(2,1)}, bf16[4,512,256]{2,1,0:T(8,128)(2,1)}) custom-call(s32[1]{0:T(128)} %bitcast.3.core_ref, bf16[4,512,512]{2,1,0:T(8,128)(2,1)} %bitcast.19), custom_call_target="tpu_custom_call" | custom-call | flops 1073741824 | bytes 4194304 | tf_op jit(solution)/shard_map/pallas_call | solution.py:129
  51.0 1.9 %collective-permute-start.5 = (bf16[4,512,256]{2,1,0:T(8,128)(2,1)}, bf16[4,512,256]{2,1,0:T(8,128)(2,1)}, u32[]{:S(2)}, u32[]{:S(2)}) collective-permute-start(bf16[4,512,256]{2,1,0:T(8,128)(2,1)} %get-tuple-element.10), channel_id=1, source_target_pairs={{0,12},{12,0},{1,13},{13,1},{2,14},{14,2},{3,15},{15,3},{4,16},{16... | collective-permute-start | bytes 3145736 | tf_op jit(solution)/shard_map/ppermute | solution.py:141
  53.0 9.4 %all-to-all-done.1 = bf16[8,12,8,512]{3,2,1,0:T(8,128)(2,1)S(1)} async-done(((bf16[8,12,8,512]{3,2,1,0:T(8,128)(2,1)}), bf16[8,12,8,512]{3,2,1,0:T(8,128)(2,1)S(1)}, u32[]{:S(2)}, u32[]{:S(2)}) %all-to-all-start.1) | async-done | bytes 786464 | tf_op jit(solution)/shard_map/all_to_all | solution.py:152
  62.4 0.1 copy_bitcast_fusion.a0.b0
  62.4 3.3 %collective-permute-start.3 = (bf16[12,64,512]{2,1,0:T(8,128)(2,1)S(1)}, bf16[12,64,512]{2,1,0:T(8,128)(2,1)S(1)}, u32[]{:S(2)}, u32[]{:S(2)}) collective-permute-start(bf16[12,64,512]{2,1,0:T(8,128)(2,1)S(1)} %copy_bitcast_fusion.a0.b0), channel_id=1, source_target_pairs={{576,0},{577,1},{578,2},{579,3},{580,4},{581,5},{582,6},{583,7},{5... | collective-permute-start | bytes 2359304 | tf_op jit(solution)/shard_map/ppermute | solution.py:162
  65.7 2.1 %collective-permute-start.2 = (bf16[12,64,512]{2,1,0:T(8,128)(2,1)S(1)}, bf16[12,64,512]{2,1,0:T(8,128)(2,1)S(1)}, u32[]{:S(2)}, u32[]{:S(2)}) collective-permute-start(bf16[12,64,512]{2,1,0:T(8,128)(2,1)S(1)} %copy_bitcast_fusion.a0.b0), channel_id=1, source_target_pairs={{24,0},{25,1},{26,2},{27,3},{28,4},{29,5},{30,6},{31,7},{32,8},{33... | collective-permute-start | bytes 2359304 | tf_op jit(solution)/shard_map/ppermute | solution.py:163
  67.9 0.0 collective-permute-done
  67.9 3.6 %collective-permute-start.1 = (bf16[12,64,512]{2,1,0:T(8,128)(2,1)S(1)}, bf16[12,64,512]{2,1,0:T(8,128)(2,1)S(1)}, u32[]{:S(2)}, u32[]{:S(2)}) collective-permute-start(bf16[12,64,512]{2,1,0:T(8,128)(2,1)S(1)} %copy_bitcast_fusion.a0.b0), channel_id=1, source_target_pairs={{192,0},{193,1},{194,2},{195,3},{196,4},{197,5},{198,6},{199,7},{2... | collective-permute-start | bytes 2359304 | tf_op jit(solution)/shard_map/ppermute | solution.py:161
  71.5 0.1 pad_add_fusion.1.at_ref
  71.6 0.1 pad_add_fusion.wanted_ref
  71.6 0.0 collective-permute-done.5.left_b
  71.6 0.0 collective-permute-done.4.right_b
  71.7 5.9 %collective-permute-done.3.a3.b3 = bf16[12,64,512]{2,1,0:T(8,128)(2,1)S(1)} collective-permute-done((bf16[12,64,512]{2,1,0:T(8,128)(2,1)S(1)}, bf16[12,64,512]{2,1,0:T(8,128)(2,1)S(1)}, u32[]{:S(2)}, u32[]{:S(2)}) %collective-permute-start.3) | collective-permute-done | bytes 786464 | tf_op jit(solution)/shard_map/ppermute | solution.py:162
  77.5 2.1 %collective-permute-done.2.a2.b2 = bf16[12,64,512]{2,1,0:T(8,128)(2,1)S(1)} collective-permute-done((bf16[12,64,512]{2,1,0:T(8,128)(2,1)S(1)}, bf16[12,64,512]{2,1,0:T(8,128)(2,1)S(1)}, u32[]{:S(2)}, u32[]{:S(2)}) %collective-permute-start.2) | collective-permute-done | bytes 786464 | tf_op jit(solution)/shard_map/ppermute | solution.py:163
  79.6 2.2 %collective-permute-done.1.a1.b1 = bf16[12,64,512]{2,1,0:T(8,128)(2,1)S(1)} collective-permute-done((bf16[12,64,512]{2,1,0:T(8,128)(2,1)S(1)}, bf16[12,64,512]{2,1,0:T(8,128)(2,1)S(1)}, u32[]{:S(2)}, u32[]{:S(2)}) %collective-permute-start.1) | collective-permute-done | bytes 786464 | tf_op jit(solution)/shard_map/ppermute | solution.py:161
  81.7 0.0 copy-start
  81.8 1.2 %copy-done = bf16[4,512,256]{2,1,0:T(8,128)(2,1)S(1)} copy-done((bf16[4,512,256]{2,1,0:T(8,128)(2,1)S(1)}, bf16[4,512,256]{2,1,0:T(8,128)(2,1)}, u32[]{:S(2)}) %copy-start) | copy-done | bytes 1048600
  83.0 6.1 %shard_map.56 = (f32[32,8,512]{2,1,0:T(8,128)S(1)}, bf16[32,8,512]{2,1,0:T(8,128)(2,1)S(1)}) custom-call(s32[8]{0:T(128)S(1)} %pad_add_fusion.wanted_ref, s32[2]{0:T(128)S(1)} %pad_add_fusion.1.at_ref, bf16[12,64,512]{2,1,0:T(8,128)(2,1)S(1)} %copy_bitcast_fusion.a0.b0, bf16[12,64,512]{2,1,0:T(8,128)(2,1)S(1)} %collective-permute-done.1.a1.b1, ...), custom_call_target="tpu_custom_call" | custom-call | flops 2147483648 | bytes 8388608 | tf_op jit(solution)/shard_map/pallas_call | solution.py:171
  89.1 1.9 %collective-permute-start.6 = (bf16[32,8,512]{2,1,0:T(8,128)(2,1)S(1)}, bf16[32,8,512]{2,1,0:T(8,128)(2,1)S(1)}, u32[]{:S(2)}, u32[]{:S(2)}) collective-permute-start(bf16[32,8,512]{2,1,0:T(8,128)(2,1)S(1)} %get-tuple-element.12), channel_id=1, source_target_pairs={{0,12},{12,0},{1,13},{13,1},{2,14},{14,2},{3,15},{15,3},{4,16},{16... | collective-permute-start | bytes 786440 | tf_op jit(solution)/shard_map/ppermute | solution.py:200
  91.1 1.5 %collective-permute-done.6 = bf16[32,8,512]{2,1,0:T(8,128)(2,1)S(1)} collective-permute-done((bf16[32,8,512]{2,1,0:T(8,128)(2,1)S(1)}, bf16[32,8,512]{2,1,0:T(8,128)(2,1)S(1)}, u32[]{:S(2)}, u32[]{:S(2)}) %collective-permute-start.6) | collective-permute-done | bytes 262176 | tf_op jit(solution)/shard_map/ppermute | solution.py:200
  92.6 0.1 add_convert_fusion
  92.6 20.5 %all_to_all.16 = bf16[32,8,512]{2,1,0:T(8,128)(2,1)S(1)} all-to-all(bf16[32,8,512]{2,1,0:T(8,128)(2,1)S(1)} %add_convert_fusion), channel_id=1, replica_groups=mesh['x'=4,'y'=8,'c'=2,'z'=12] {'x','y'}, dimensions={0} | all-to-all | bytes 524288 | tf_op jit(solution)/shard_map/all_to_all | solution.py:201
  113.2 0.7 fusion
  (4 shorter events, 0.1 us)
Async XLA Ops:
  0.0 44.0 %copy-start.1 = (s32[4,1]{0,1:T(1,128)S(1)}, s32[4,1]{0,1:T(1,128)}, u32[]{:S(2)}) copy-start(s32[4,1]{0,1:T(1,128)} %param.9) | copy-start | bytes 52
  32.9 29.4 %all-to-all-start.1 = ((bf16[8,12,8,512]{3,2,1,0:T(8,128)(2,1)}), bf16[8,12,8,512]{3,2,1,0:T(8,128)(2,1)S(1)}, u32[]{:S(2)}, u32[]{:S(2)}) async-start(bf16[8,12,8,512]{3,2,1,0:T(8,128)(2,1)} %broadcast_in_dim.28), calls=%async_computation.1 | async-start | bytes 1572864 | tf_op jit(solution)/shard_map/all_to_all | solution.py:152
  42.1 29.6 %collective-permute-start.4 = (bf16[4,512,512]{2,1,0:T(8,128)(2,1)}, bf16[4,512,512]{2,1,0:T(8,128)(2,1)}, u32[]{:S(2)}, u32[]{:S(2)}) collective-permute-start(bf16[4,512,512]{2,1,0:T(8,128)(2,1)} %bitcast.7.right_a), channel_id=1, source_target_pairs={{0,12},{12,0},{1,13},{13,1},{2,14},{14,2},{3,15},{15,3},{4,16},{16... | collective-permute-start | bytes 6291464 | tf_op jit(solution)/shard_map/ppermute | solution.py:140
  44.0 23.8 %collective-permute-start = (s32[4]{0:T(128)S(1)}, s32[4]{0:T(128)S(1)}, u32[]{:S(2)}, u32[]{:S(2)}) collective-permute-start(s32[4]{0:T(128)S(1)} %bitcast.20), channel_id=1, source_target_pairs={{0,12},{12,0},{1,13},{13,1},{2,14},{14,2},{3,15},{15,3},{4,16},{16... | collective-permute-start | bytes 56 | tf_op jit(solution)/shard_map/ppermute | solution.py:142
  51.0 20.6 %collective-permute-start.5 = (bf16[4,512,256]{2,1,0:T(8,128)(2,1)}, bf16[4,512,256]{2,1,0:T(8,128)(2,1)}, u32[]{:S(2)}, u32[]{:S(2)}) collective-permute-start(bf16[4,512,256]{2,1,0:T(8,128)(2,1)} %get-tuple-element.10), channel_id=1, source_target_pairs={{0,12},{12,0},{1,13},{13,1},{2,14},{14,2},{3,15},{15,3},{4,16},{16... | collective-permute-start | bytes 3145736 | tf_op jit(solution)/shard_map/ppermute | solution.py:141
  62.4 15.1 %collective-permute-start.3 = (bf16[12,64,512]{2,1,0:T(8,128)(2,1)S(1)}, bf16[12,64,512]{2,1,0:T(8,128)(2,1)S(1)}, u32[]{:S(2)}, u32[]{:S(2)}) collective-permute-start(bf16[12,64,512]{2,1,0:T(8,128)(2,1)S(1)} %copy_bitcast_fusion.a0.b0), channel_id=1, source_target_pairs={{576,0},{577,1},{578,2},{579,3},{580,4},{581,5},{582,6},{583,7},{5... | collective-permute-start | bytes 2359304 | tf_op jit(solution)/shard_map/ppermute | solution.py:162
  65.7 13.9 %collective-permute-start.2 = (bf16[12,64,512]{2,1,0:T(8,128)(2,1)S(1)}, bf16[12,64,512]{2,1,0:T(8,128)(2,1)S(1)}, u32[]{:S(2)}, u32[]{:S(2)}) collective-permute-start(bf16[12,64,512]{2,1,0:T(8,128)(2,1)S(1)} %copy_bitcast_fusion.a0.b0), channel_id=1, source_target_pairs={{24,0},{25,1},{26,2},{27,3},{28,4},{29,5},{30,6},{31,7},{32,8},{33... | collective-permute-start | bytes 2359304 | tf_op jit(solution)/shard_map/ppermute | solution.py:163
  67.9 13.9 %collective-permute-start.1 = (bf16[12,64,512]{2,1,0:T(8,128)(2,1)S(1)}, bf16[12,64,512]{2,1,0:T(8,128)(2,1)S(1)}, u32[]{:S(2)}, u32[]{:S(2)}) collective-permute-start(bf16[12,64,512]{2,1,0:T(8,128)(2,1)S(1)} %copy_bitcast_fusion.a0.b0), channel_id=1, source_target_pairs={{192,0},{193,1},{194,2},{195,3},{196,4},{197,5},{198,6},{199,7},{2... | collective-permute-start | bytes 2359304 | tf_op jit(solution)/shard_map/ppermute | solution.py:161
  81.7 1.2 %copy-start = (bf16[4,512,256]{2,1,0:T(8,128)(2,1)S(1)}, bf16[4,512,256]{2,1,0:T(8,128)(2,1)}, u32[]{:S(2)}) copy-start(bf16[4,512,256]{2,1,0:T(8,128)(2,1)} %get-tuple-element.9.left_a) | copy-start | bytes 3145732
  89.1 3.4 %collective-permute-start.6 = (bf16[32,8,512]{2,1,0:T(8,128)(2,1)S(1)}, bf16[32,8,512]{2,1,0:T(8,128)(2,1)S(1)}, u32[]{:S(2)}, u32[]{:S(2)}) collective-permute-start(bf16[32,8,512]{2,1,0:T(8,128)(2,1)S(1)} %get-tuple-element.12), channel_id=1, source_target_pairs={{0,12},{12,0},{1,13},{13,1},{2,14},{14,2},{3,15},{15,3},{4,16},{16... | collective-permute-start | bytes 786440 | tf_op jit(solution)/shard_map/ppermute | solution.py:200

commit v2 on v1

v2 whole, which is shorter than its diff:
```python
import functools

import jax
import jax.numpy as jnp
from jax import lax
from jax.experimental import pallas as pl
from jax.experimental.pallas import tpu as pltpu
from jax.sharding import Mesh
from jax.sharding import PartitionSpec as P

NX, NY, NC, NZ = 4, 8, 2, 12
B = 512
ROWS = 8
HALF = B // 2
UNIT = 2 * ROWS
CHIP = ("x", "y")
ALL = ("x", "y", "c", "z")


def far_groups():
    return [
        [((g - z) % 4 + 4 * half) * NZ + z for z in range(NZ) for half in range(2)]
        for g in range(4)
    ]


def near_groups():
    return [
        [(x * NY + (y + x % 2) % NY) * NZ + (z + x % 2) % NZ for x in range(NX)]
        for y in range(NY)
        for z in range(NZ)
    ]


def shifts(core0, core1):
    pairs = []
    for x in range(NX):
        for y in range(NY):
            for c in range(NC):
                for z in range(NZ):
                    dx, dy, dz = core0 if c == 0 else core1
                    at = ((x * NY + y) * NC + c) * NZ + z
                    come = (((x + dx) % NX * NY + (y + dy) % NY) * NC + c) * NZ + (z + dz) % NZ
                    pairs.append((come, at))
    return pairs


def split_columns(core_ref, left_ref, own_ref, other_ref):
    core = core_ref[0]
    row = lax.broadcasted_iota(jnp.int32, (B, B), 0)
    col = lax.broadcasted_iota(jnp.int32, (B, B), 1)
    where_from = (
        ((col >> 6) & 3) * 128
        + ((col >> 3) & 1) * 64
        + ((col >> 4) & 3) * 16
        + (((col >> 8) & 1) ^ core) * 8
        + (col & 7)
    )
    pick = jnp.where(row == where_from, 1.0, 0.0).astype(jnp.bfloat16)
    moved = jnp.dot(left_ref[0], pick, preferred_element_type=jnp.float32).astype(jnp.bfloat16)
    own_ref[...] = moved[:, :HALF]
    other_ref[...] = moved[:, HALF:]


def partial_sum(
    quarters, wanted_ref, wanted_far_ref, at_ref, parts, right_ref, right_far_ref, left_ref, left_far_ref, product
):
    terms = right_ref.shape[0]
    rest = [q for q in range(4) if q not in quarters]
    zeros = jnp.zeros((UNIT, B), jnp.bfloat16)

    def multiply(sector, right, slot):
        start = at_ref[0] + 16 - sector
        rows = jnp.concatenate([p[x, sector] for p in parts for x in range(NX)], axis=0)
        result = jnp.dot(rows, right, preferred_element_type=jnp.float32).astype(jnp.bfloat16)
        base = slot * (HALF // UNIT)
        for i, q in enumerate(quarters):
            for x in range(NX):
                at = (i * NX + x) * UNIT
                product[base + x * 4 + ((start + q - 2 * x) & 3)] = result[at : at + UNIT]
        for q in rest:
            for x in range(NX):
                product[base + x * 4 + ((start + q - 2 * x) & 3)] = zeros

    for k in range(terms):
        multiply(wanted_ref[k], right_ref[k], k)
        multiply(wanted_far_ref[k], right_far_ref[k], terms + k)
    middle = terms * HALF // UNIT
    return jnp.dot(
        left_ref[...],
        product[:middle].reshape(terms * HALF, B),
        preferred_element_type=jnp.float32,
    ) + jnp.dot(
        left_far_ref[...],
        product[middle:].reshape(terms * HALF, B),
        preferred_element_type=jnp.float32,
    )


def early_sum(
    wanted_ref, wanted_far_ref, at_ref, part0, part3, right_ref, right_far_ref, left_ref, left_far_ref, total_ref, product
):
    total_ref[...] = partial_sum(
        (0, 3), wanted_ref, wanted_far_ref, at_ref, (part0, part3), right_ref, right_far_ref, left_ref, left_far_ref, product
    )


def late_sum(
    wanted_ref, wanted_far_ref, at_ref, part1, part2, right_ref, right_far_ref, left_ref, left_far_ref, early_ref, keep_ref, send_ref, product
):
    total = early_ref[...] + partial_sum(
        (1, 2), wanted_ref, wanted_far_ref, at_ref, (part1, part2), right_ref, right_far_ref, left_ref, left_far_ref, product
    )
    pairs = total.reshape(NX * NY, 2, ROWS, B)
    low, high = pairs[:, 0], pairs[:, 1]
    first = at_ref[1] == 0
    keep_ref[...] = jnp.where(first, low, high)
    send_ref[...] = jnp.where(first, high, low).astype(jnp.bfloat16)


def on_device(psi, sizes, left_ops, right_ops, source):
    x, y, c, z = (lax.axis_index(a) for a in ALL)
    term_count = left_ops.shape[0]
    swap = [(0, 1), (1, 0)]
    left = left_ops.reshape(term_count, B, B)
    right = right_ops.reshape(term_count, B, B)
    wanted = source.reshape(term_count)

    own_rows = ((x * NY + y) * NC + c) * ROWS + jnp.arange(ROWS, dtype=jnp.int32)
    columns = jnp.arange(B, dtype=jnp.int32)
    inside = (own_rows[:, None] < sizes[0]) & (columns[None, :] < sizes[0])
    masked = jnp.where(inside, psi[0], jnp.zeros((), psi.dtype))

    core = c.astype(jnp.int32).reshape(1)
    left_own, left_other = pl.pallas_call(
        split_columns,
        grid_spec=pltpu.PrefetchScalarGridSpec(
            num_scalar_prefetch=1,
            grid=(term_count,),
            in_specs=[pl.BlockSpec((1, B, B), lambda k, core: (k, 0, 0))],
            out_specs=[pl.BlockSpec((B, HALF), lambda k, core: (0, k))] * 2,
        ),
        out_shape=[jax.ShapeDtypeStruct((B, term_count * HALF), jnp.bfloat16)] * 2,
        cost_estimate=pl.CostEstimate(flops=2 * term_count * B**3, bytes_accessed=4 * term_count * B * B, transcendentals=0),
    )(core, left)
    right_far = lax.ppermute(right, "c", swap)
    wanted_far = lax.ppermute(wanted, "c", swap)

    far = lax.all_to_all(
        jnp.broadcast_to(masked[None], (2 * NZ, ROWS, B)),
        ("y", "z"),
        0,
        0,
        axis_index_groups=far_groups(),
        tiled=True,
    ).reshape(NZ, UNIT, B)
    far, left_own, left_other, wanted_far = lax.optimization_barrier(
        (far, left_own, left_other, wanted_far)
    )
    left_far = lax.ppermute(left_other, "c", swap)
    part = lax.all_to_all(
        jnp.broadcast_to(far[None], (NX, NZ, UNIT, B)),
        ("x", "y", "z"),
        0,
        0,
        axis_index_groups=near_groups(),
        tiled=True,
    )
    up = lax.ppermute(part, ALL, shifts((0, 1, 0), (0, 0, 1)))
    down = lax.ppermute(part, ALL, shifts((0, -1, 0), (0, 0, -1)))
    across = lax.ppermute(part, ALL, shifts((1, 0, 0), (-1, 0, 0)))

    in_smem = pl.BlockSpec(memory_space=pltpu.SMEM)
    in_vmem = pl.BlockSpec(memory_space=pltpu.VMEM)
    settings = dict(
        scratch_shapes=[pltpu.VMEM((2 * term_count * HALF // UNIT, UNIT, B), jnp.bfloat16)],
        compiler_params=pltpu.CompilerParams(vmem_limit_bytes=16 * 1024 * 1024),
        cost_estimate=pl.CostEstimate(
            flops=4 * term_count * HALF * B * B,
            bytes_accessed=16 * term_count * HALF * B,
            transcendentals=0,
        ),
    )
    at = jnp.stack([(2 * x + y + z).astype(jnp.int32), c.astype(jnp.int32)])
    early = pl.pallas_call(
        early_sum,
        in_specs=[in_smem] * 3 + [in_vmem] * 6,
        out_specs=in_vmem,
        out_shape=jax.ShapeDtypeStruct((B, B), jnp.float32),
        **settings,
    )(wanted, wanted_far, at, part, down, right, right_far, left_own, left_far)
    keep, send = pl.pallas_call(
        late_sum,
        in_specs=[in_smem] * 3 + [in_vmem] * 7,
        out_specs=[in_vmem] * 2,
        out_shape=[
            jax.ShapeDtypeStruct((NX * NY, ROWS, B), jnp.float32),
            jax.ShapeDtypeStruct((NX * NY, ROWS, B), jnp.bfloat16),
        ],
        **settings,
    )(wanted, wanted_far, at, up, across, right, right_far, left_own, left_far, early)
    chip_sum = keep + lax.ppermute(send, "c", swap).astype(jnp.float32)
    shares = lax.all_to_all(chip_sum.astype(jnp.bfloat16), CHIP, 0, 0, tiled=True)
    summed = jnp.sum(shares.astype(jnp.float32), axis=0)
    return jnp.where(inside, summed, jnp.float32(0.0)).astype(jnp.bfloat16)[:, None, :]


def solution(mesh):
    fine = Mesh(mesh.devices.reshape(NX, NY, NC, NZ), ALL)
    term = ("x", "y", "c")
    return jax.shard_map(
        on_device,
        mesh=fine,
        in_specs=(
            P("z", term, None),
            P("z"),
            P(term, "z", None, None),
            P(term, "z", None, None),
            P(term, "z"),
        ),
        out_specs=P(term, "z", None),
        check_vma=False,
    )
```

time: 115 us -> 108 us (0.939)
  blocking collectives: 51 us -> 22.3 us
  starting transfers between devices: 26.3 us -> 43 us
  waiting for transfers between devices: 21 us -> 24.4 us
  Pallas kernels: 10.8 us -> 12.6 us
    all_to_all x1 -> x0, blocking collectives: 30.5 us -> none  [on_device(): lax.all_to_all(jnp.broadcast_to(masked[None], (NZ, ROWS, B)), ('x', 'z'),...]
    all_to_all x1 -> x2, starting transfers between devices: 9.17 us -> 23.2 us  [the longest x1 18.9 us: on_device(): lax.all_to_all(jnp.broadcast_to(masked[None], (2 * NZ, ROWS, B)), ('y', '...]
    all_to_all x1 -> x2, waiting for transfers between devices: 9.39 us -> 18 us  [the longest x1 11 us: on_device(): lax.all_to_all(jnp.broadcast_to(masked[None], (2 * NZ, ROWS, B)), ('y', '...]
    ppermute x3, waiting for transfers between devices: 10.1 us -> 4.88 us  [the longest x1 2.69 us: on_device(): down = lax.ppermute(part, ALL, shifts((0, -1, 0), (0, 0, -1)))]
    ppermute x3, starting transfers between devices: 9 us -> 11.6 us  [the longest x1 5.54 us: on_device(): across = lax.ppermute(part, ALL, shifts((1, 0, 0), (-1, 0, 0)))]
    pallas_call x1 -> x2, Pallas kernels: 6.14 us -> 7.9 us  [the longest x1 3.96 us: on_device(): pl.pallas_call(late_sum, in_specs=[in_smem] * 3 + [in_vmem] * 7, out_spec...]
    all_to_all x1, blocking collectives: 20.5 us -> 22.3 us  [on_device(): lax.all_to_all(chip_sum.astype(jnp.bfloat16), CHIP, 0, 0, tiled=True)]
  transfers between devices with their start and end apart: 8 -> 9, of which waited for: 5 -> 5; matrix products, arithmetic and copies ran while one was open for 0% -> 0% of each run, Pallas kernels for 4% -> 8%
where the time goes in v2:
time: 108 us
  starting transfers between devices  43 us (40%)
  waiting for transfers between devices  24.4 us (23%)
  blocking collectives  22.3 us (21%)
  Pallas kernels  12.6 us (12%)
  local copies, waits for them, and re-layouts  2.94 us (3%)
  other arithmetic  1.66 us (2%)
    all_to_all x1, blocking collectives, on_device(): lax.all_to_all(chip_sum.astype(jnp.bfloat16), CHIP, 0, 0, tiled=True)  22.3 us
    all_to_all x1, starting transfers between devices, on_device(): lax.all_to_all(jnp.broadcast_to(masked[None], (2 * NZ, ROWS, B)), ('y', '...  18.9 us
    all_to_all x1, waiting for transfers between devices, on_device(): lax.all_to_all(jnp.broadcast_to(masked[None], (2 * NZ, ROWS, B)), ('y', '...  11 us
    all_to_all x1, waiting for transfers between devices, on_device(): lax.all_to_all(jnp.broadcast_to(far[None], (NX, NZ, UNIT, B)), ('x', 'y',...  7.04 us
    ppermute x1, starting transfers between devices, on_device(): across = lax.ppermute(part, ALL, shifts((1, 0, 0), (-1, 0, 0)))  5.54 us
    pallas_call x1, Pallas kernels, on_device(): pl.pallas_call(split_columns, grid_spec=pltpu.PrefetchScalarGridSpec(num_...  4.68 us
    all_to_all x1, starting transfers between devices, on_device(): lax.all_to_all(jnp.broadcast_to(far[None], (NX, NZ, UNIT, B)), ('x', 'y',...  4.29 us
    ppermute x1, starting transfers between devices, on_device(): up = lax.ppermute(part, ALL, shifts((0, 1, 0), (0, 0, 1)))  4.11 us
  transfers between devices with their start and end apart: 9, of which 5 were waited for; matrix products, arithmetic and copies ran while one was open for 0% of the time, Pallas kernels for 8%

profile of v2, /device:TPU:8, one launch (start us, length us, event | category | flops | bytes accessed | tf_op | source)
XLA Modules:
  0.0 107.6 jit_solution(622095477617811327)
XLA Ops:
  0.7 0.8 fusion.1
  1.5 0.7 broadcast_in_dim.27
  2.1 18.9 %all-to-all-start = ((bf16[24,8,512]{2,1,0:T(8,128)(2,1)}), bf16[24,8,512]{2,1,0:T(8,128)(2,1)S(1)}, u32[]{:S(2)}, u32[]{:S(2)}) async-start(bf16[24,8,512]{2,1,0:T(8,128)(2,1)} %broadcast_in_dim.27), calls=%async_computation | async-start | bytes 393216 | tf_op jit(solution)/shard_map/all_to_all | solution.py:149
  21.1 1.9 %collective-permute-start = (s32[4]{0:T(128)}, s32[4]{0:T(128)S(1)}, u32[]{:S(2)}, u32[]{:S(2)}) collective-permute-start(s32[4]{0:T(128)} %bitcast.18), channel_id=1, source_target_pairs={{0,12},{12,0},{1,13},{13,1},{2,14},{14,2},{3,15},{15,3},{4,16},{16... | collective-permute-start | bytes 56 | tf_op jit(solution)/shard_map/ppermute | solution.py:147
  23.0 4.7 %shard_map.55 = (bf16[512,1024]{1,0:T(8,128)(2,1)}, bf16[512,1024]{1,0:T(8,128)(2,1)}) custom-call(s32[1]{0:T(128)} %bitcast.4.core_ref, bf16[4,512,512]{2,1,0:T(8,128)(2,1)} %bitcast.22), custom_call_target="tpu_custom_call" | custom-call | flops 1073741824 | bytes 4194304 | tf_op jit(solution)/shard_map/pallas_call | solution.py:135
  27.7 0.0 copy-start
  27.7 0.0 copy-start.2
  27.7 0.0 collective-permute-done.wanted_far_ref
  27.7 11.0 %all-to-all-done = bf16[24,8,512]{2,1,0:T(8,128)(2,1)S(1)} async-done(((bf16[24,8,512]{2,1,0:T(8,128)(2,1)}), bf16[24,8,512]{2,1,0:T(8,128)(2,1)S(1)}, u32[]{:S(2)}, u32[]{:S(2)}) %all-to-all-start) | async-done | bytes 196640 | tf_op jit(solution)/shard_map/all_to_all | solution.py:149
  38.7 1.0 broadcast_in_dim.28
  39.7 4.3 %all-to-all-start.1 = ((bf16[4,12,16,512]{3,2,1,0:T(8,128)(2,1)}), bf16[4,12,16,512]{3,2,1,0:T(8,128)(2,1)}, u32[]{:S(2)}, u32[]{:S(2)}) async-start(bf16[4,12,16,512]{3,2,1,0:T(8,128)(2,1)} %broadcast_in_dim.28), calls=%async_computation.1 | async-start | bytes 1572864 | tf_op jit(solution)/shard_map/all_to_all | solution.py:161
  44.0 0.0 copy-done
  44.0 1.9 %collective-permute-start.3 = (bf16[4,512,512]{2,1,0:T(8,128)(2,1)S(1)}, bf16[4,512,512]{2,1,0:T(8,128)(2,1)}, u32[]{:S(2)}, u32[]{:S(2)}) collective-permute-start(bf16[4,512,512]{2,1,0:T(8,128)(2,1)S(1)} %bitcast.15), channel_id=1, source_target_pairs={{0,12},{12,0},{1,13},{13,1},{2,14},{14,2},{3,15},{15,3},{4,16},{16... | collective-permute-start | bytes 6291464 | tf_op jit(solution)/shard_map/ppermute | solution.py:146
  45.9 2.4 %collective-permute-start.4 = (bf16[512,1024]{1,0:T(8,128)(2,1)}, bf16[512,1024]{1,0:T(8,128)(2,1)S(1)}, u32[]{:S(2)}, u32[]{:S(2)}) collective-permute-start(bf16[512,1024]{1,0:T(8,128)(2,1)} %get-tuple-element.18), channel_id=1, source_target_pairs={{0,12},{12,0},{1,13},{13,1},{2,14},{14,2},{3,15},{15,3},{4,16},{16... | collective-permute-start | bytes 3145736 | tf_op jit(solution)/shard_map/ppermute | solution.py:160
  48.3 7.0 %all-to-all-done.1.part0 = bf16[4,12,16,512]{3,2,1,0:T(8,128)(2,1)} async-done(((bf16[4,12,16,512]{3,2,1,0:T(8,128)(2,1)}), bf16[4,12,16,512]{3,2,1,0:T(8,128)(2,1)}, u32[]{:S(2)}, u32[]{:S(2)}) %all-to-all-start.1) | async-done | bytes 786464 | tf_op jit(solution)/shard_map/all_to_all | solution.py:161
  55.4 1.9 %collective-permute-start.5 = (bf16[4,12,16,512]{3,2,1,0:T(8,128)(2,1)}, bf16[4,12,16,512]{3,2,1,0:T(8,128)(2,1)}, u32[]{:S(2)}, u32[]{:S(2)}) collective-permute-start(bf16[4,12,16,512]{3,2,1,0:T(8,128)(2,1)} %all-to-all-done.1.part0), channel_id=1, source_target_pairs={{168,0},{169,1},{170,2},{171,3},{172,4},{173,5},{174,6},{175,7},{1... | collective-permute-start | bytes 2359304 | tf_op jit(solution)/shard_map/ppermute | solution.py:170
  57.3 4.1 %collective-permute-start.1 = (bf16[4,12,16,512]{3,2,1,0:T(8,128)(2,1)}, bf16[4,12,16,512]{3,2,1,0:T(8,128)(2,1)}, u32[]{:S(2)}, u32[]{:S(2)}) collective-permute-start(bf16[4,12,16,512]{3,2,1,0:T(8,128)(2,1)} %all-to-all-done.1.part0), channel_id=1, source_target_pairs={{24,0},{25,1},{26,2},{27,3},{28,4},{29,5},{30,6},{31,7},{32,8},{33... | collective-permute-start | bytes 2359304 | tf_op jit(solution)/shard_map/ppermute | solution.py:169
  61.4 5.5 %collective-permute-start.2 = (bf16[4,12,16,512]{3,2,1,0:T(8,128)(2,1)}, bf16[4,12,16,512]{3,2,1,0:T(8,128)(2,1)}, u32[]{:S(2)}, u32[]{:S(2)}) collective-permute-start(bf16[4,12,16,512]{3,2,1,0:T(8,128)(2,1)} %all-to-all-done.1.part0), channel_id=1, source_target_pairs={{192,0},{193,1},{194,2},{195,3},{196,4},{197,5},{198,6},{199,7},{2... | collective-permute-start | bytes 2359304 | tf_op jit(solution)/shard_map/ppermute | solution.py:171
  67.0 0.1 pad_add_fusion.at_ref
  67.0 0.0 collective-permute-done.4.left_far_ref
  67.0 0.0 collective-permute-done.3.right_far_ref
  67.0 2.7 %collective-permute-done.5.part3 = bf16[4,12,16,512]{3,2,1,0:T(8,128)(2,1)} collective-permute-done((bf16[4,12,16,512]{3,2,1,0:T(8,128)(2,1)}, bf16[4,12,16,512]{3,2,1,0:T(8,128)(2,1)}, u32[]{:S(2)}, u32[]{:S(2)}) %collective-permute-start.5) | collective-permute-done | bytes 786464 | tf_op jit(solution)/shard_map/ppermute | solution.py:170
  69.7 0.0 copy-done.2
  69.7 0.0 copy-start.1
  69.7 1.2 %copy-done.1 = bf16[512,1024]{1,0:T(8,128)(2,1)S(1)} copy-done((bf16[512,1024]{1,0:T(8,128)(2,1)S(1)}, bf16[512,1024]{1,0:T(8,128)(2,1)}, u32[]{:S(2)}) %copy-start.1) | copy-done | bytes 1048600
  71.0 3.9 %shard_map.56.early_ref = f32[512,512]{1,0:T(8,128)S(1)} custom-call(s32[4]{0:T(128)S(1)} %bitcast.19, s32[4]{0:T(128)S(1)} %collective-permute-done.wanted_far_ref, s32[2]{0:T(128)S(1)} %pad_add_fusion.at_ref, bf16[4,12,16,512]{3,2,1,0:T(8,128)(2,1)} %all-to-all-done.1.part0, bf16[4,12,16,512]{3,2,1,0:T(8,128)(2,1)} %collective-permute-done.5.part3, ...), custom_call_target="tpu_custom_call" | custom-call | flops 1073741824 | bytes 8388608 | tf_op jit(solution)/shard_map/pallas_call | solution.py:185
  74.9 0.0 collective-permute-done.1.part1
  74.9 2.2 %collective-permute-done.2.part2 = bf16[4,12,16,512]{3,2,1,0:T(8,128)(2,1)} collective-permute-done((bf16[4,12,16,512]{3,2,1,0:T(8,128)(2,1)}, bf16[4,12,16,512]{3,2,1,0:T(8,128)(2,1)}, u32[]{:S(2)}, u32[]{:S(2)}) %collective-permute-start.2) | collective-permute-done | bytes 786464 | tf_op jit(solution)/shard_map/ppermute | solution.py:171
  77.1 4.0 %shard_map.57 = (f32[32,8,512]{2,1,0:T(8,128)S(1)}, bf16[32,8,512]{2,1,0:T(8,128)(2,1)S(1)}) custom-call(s32[4]{0:T(128)S(1)} %bitcast.20, s32[4]{0:T(128)S(1)} %collective-permute-done.wanted_far_ref, s32[2]{0:T(128)S(1)} %pad_add_fusion.at_ref, bf16[4,12,16,512]{3,2,1,0:T(8,128)(2,1)} %collective-permute-done.1.part1, ...), custom_call_target="tpu_custom_call" | custom-call | flops 1073741824 | bytes 8388608 | tf_op jit(solution)/shard_map/pallas_call | solution.py:192
  81.1 1.9 %collective-permute-start.6 = (bf16[32,8,512]{2,1,0:T(8,128)(2,1)S(1)}, bf16[32,8,512]{2,1,0:T(8,128)(2,1)S(1)}, u32[]{:S(2)}, u32[]{:S(2)}) collective-permute-start(bf16[32,8,512]{2,1,0:T(8,128)(2,1)S(1)} %get-tuple-element.20), channel_id=1, source_target_pairs={{0,12},{12,0},{1,13},{13,1},{2,14},{14,2},{3,15},{15,3},{4,16},{16... | collective-permute-start | bytes 786440 | tf_op jit(solution)/shard_map/ppermute | solution.py:202
  83.0 1.5 %collective-permute-done.6 = bf16[32,8,512]{2,1,0:T(8,128)(2,1)S(1)} collective-permute-done((bf16[32,8,512]{2,1,0:T(8,128)(2,1)S(1)}, bf16[32,8,512]{2,1,0:T(8,128)(2,1)S(1)}, u32[]{:S(2)}, u32[]{:S(2)}) %collective-permute-start.6) | collective-permute-done | bytes 262176 | tf_op jit(solution)/shard_map/ppermute | solution.py:202
  84.5 0.1 add_convert_fusion
  84.6 22.3 %all_to_all.15 = bf16[32,8,512]{2,1,0:T(8,128)(2,1)S(1)} all-to-all(bf16[32,8,512]{2,1,0:T(8,128)(2,1)S(1)} %add_convert_fusion), channel_id=1, replica_groups=mesh['x'=4,'y'=8,'c'=2,'z'=12] {'x','y'}, dimensions={0} | all-to-all | bytes 524288 | tf_op jit(solution)/shard_map/all_to_all | solution.py:203
  106.9 0.7 fusion
  (3 shorter events, 0.1 us)
Async XLA Ops:
  2.1 36.5 %all-to-all-start = ((bf16[24,8,512]{2,1,0:T(8,128)(2,1)}), bf16[24,8,512]{2,1,0:T(8,128)(2,1)S(1)}, u32[]{:S(2)}, u32[]{:S(2)}) async-start(bf16[24,8,512]{2,1,0:T(8,128)(2,1)} %broadcast_in_dim.27), calls=%async_computation | async-start | bytes 393216 | tf_op jit(solution)/shard_map/all_to_all | solution.py:149
  21.1 6.6 %collective-permute-start = (s32[4]{0:T(128)}, s32[4]{0:T(128)S(1)}, u32[]{:S(2)}, u32[]{:S(2)}) collective-permute-start(s32[4]{0:T(128)} %bitcast.18), channel_id=1, source_target_pairs={{0,12},{12,0},{1,13},{13,1},{2,14},{14,2},{3,15},{15,3},{4,16},{16... | collective-permute-start | bytes 56 | tf_op jit(solution)/shard_map/ppermute | solution.py:147
  27.7 16.3 %copy-start = (bf16[4,1,512,512]{3,2,1,0:T(8,128)(2,1)S(1)}, bf16[4,1,512,512]{3,2,1,0:T(8,128)(2,1)}, u32[]{:S(2)}) copy-start(bf16[4,1,512,512]{3,2,1,0:T(8,128)(2,1)} %param.8) | copy-start | bytes 6291460
  27.7 42.0 %copy-start.2 = (s32[4,1]{0,1:T(1,128)S(1)}, s32[4,1]{0,1:T(1,128)}, u32[]{:S(2)}) copy-start(s32[4,1]{0,1:T(1,128)} %param.9) | copy-start | bytes 52
  39.7 15.7 %all-to-all-start.1 = ((bf16[4,12,16,512]{3,2,1,0:T(8,128)(2,1)}), bf16[4,12,16,512]{3,2,1,0:T(8,128)(2,1)}, u32[]{:S(2)}, u32[]{:S(2)}) async-start(bf16[4,12,16,512]{3,2,1,0:T(8,128)(2,1)} %broadcast_in_dim.28), calls=%async_computation.1 | async-start | bytes 1572864 | tf_op jit(solution)/shard_map/all_to_all | solution.py:161
  44.0 23.1 %collective-permute-start.3 = (bf16[4,512,512]{2,1,0:T(8,128)(2,1)S(1)}, bf16[4,512,512]{2,1,0:T(8,128)(2,1)}, u32[]{:S(2)}, u32[]{:S(2)}) collective-permute-start(bf16[4,512,512]{2,1,0:T(8,128)(2,1)S(1)} %bitcast.15), channel_id=1, source_target_pairs={{0,12},{12,0},{1,13},{13,1},{2,14},{14,2},{3,15},{15,3},{4,16},{16... | collective-permute-start | bytes 6291464 | tf_op jit(solution)/shard_map/ppermute | solution.py:146
  45.9 21.1 %collective-permute-start.4 = (bf16[512,1024]{1,0:T(8,128)(2,1)}, bf16[512,1024]{1,0:T(8,128)(2,1)S(1)}, u32[]{:S(2)}, u32[]{:S(2)}) collective-permute-start(bf16[512,1024]{1,0:T(8,128)(2,1)} %get-tuple-element.18), channel_id=1, source_target_pairs={{0,12},{12,0},{1,13},{13,1},{2,14},{14,2},{3,15},{15,3},{4,16},{16... | collective-permute-start | bytes 3145736 | tf_op jit(solution)/shard_map/ppermute | solution.py:160
  55.4 14.4 %collective-permute-start.5 = (bf16[4,12,16,512]{3,2,1,0:T(8,128)(2,1)}, bf16[4,12,16,512]{3,2,1,0:T(8,128)(2,1)}, u32[]{:S(2)}, u32[]{:S(2)}) collective-permute-start(bf16[4,12,16,512]{3,2,1,0:T(8,128)(2,1)} %all-to-all-done.1.part0), channel_id=1, source_target_pairs={{168,0},{169,1},{170,2},{171,3},{172,4},{173,5},{174,6},{175,7},{1... | collective-permute-start | bytes 2359304 | tf_op jit(solution)/shard_map/ppermute | solution.py:170
  57.3 17.6 %collective-permute-start.1 = (bf16[4,12,16,512]{3,2,1,0:T(8,128)(2,1)}, bf16[4,12,16,512]{3,2,1,0:T(8,128)(2,1)}, u32[]{:S(2)}, u32[]{:S(2)}) collective-permute-start(bf16[4,12,16,512]{3,2,1,0:T(8,128)(2,1)} %all-to-all-done.1.part0), channel_id=1, source_target_pairs={{24,0},{25,1},{26,2},{27,3},{28,4},{29,5},{30,6},{31,7},{32,8},{33... | collective-permute-start | bytes 2359304 | tf_op jit(solution)/shard_map/ppermute | solution.py:169
  61.4 15.7 %collective-permute-start.2 = (bf16[4,12,16,512]{3,2,1,0:T(8,128)(2,1)}, bf16[4,12,16,512]{3,2,1,0:T(8,128)(2,1)}, u32[]{:S(2)}, u32[]{:S(2)}) collective-permute-start(bf16[4,12,16,512]{3,2,1,0:T(8,128)(2,1)} %all-to-all-done.1.part0), channel_id=1, source_target_pairs={{192,0},{193,1},{194,2},{195,3},{196,4},{197,5},{198,6},{199,7},{2... | collective-permute-start | bytes 2359304 | tf_op jit(solution)/shard_map/ppermute | solution.py:171
  69.7 1.2 %copy-start.1 = (bf16[512,1024]{1,0:T(8,128)(2,1)S(1)}, bf16[512,1024]{1,0:T(8,128)(2,1)}, u32[]{:S(2)}) copy-start(bf16[512,1024]{1,0:T(8,128)(2,1)} %get-tuple-element.17.left_ref) | copy-start | bytes 3145732
  81.1 3.4 %collective-permute-start.6 = (bf16[32,8,512]{2,1,0:T(8,128)(2,1)S(1)}, bf16[32,8,512]{2,1,0:T(8,128)(2,1)S(1)}, u32[]{:S(2)}, u32[]{:S(2)}) collective-permute-start(bf16[32,8,512]{2,1,0:T(8,128)(2,1)S(1)} %get-tuple-element.20), channel_id=1, source_target_pairs={{0,12},{12,0},{1,13},{13,1},{2,14},{14,2},{3,15},{15,3},{4,16},{16... | collective-permute-start | bytes 786440 | tf_op jit(solution)/shard_map/ppermute | solution.py:202

commit v3 on v2

--- a/solution.py
+++ b/solution.py
@@ -62,55 +62,89 @@
     other_ref[...] = moved[:, HALF:]
 
 
-def partial_sum(
-    quarters, wanted_ref, wanted_far_ref, at_ref, parts, right_ref, right_far_ref, left_ref, left_far_ref, product
+def multiply(quarters, parts, sector, start, right, product, slot):
+    rows = jnp.concatenate([p[x, sector] for p in parts for x in range(NX)], axis=0)
+    result = jnp.dot(rows, right, preferred_element_type=jnp.float32).astype(jnp.bfloat16)
+    for i, q in enumerate(quarters):
+        for x in range(NX):
+            at = (i * NX + x) * UNIT
+            place = slot * (HALF // UNIT) + x * 4 + ((start + q - 2 * x) & 3)
+            product[place] = result[at : at + UNIT]
+
+
+def early_products(
+    wanted_ref,
+    wanted_far_ref,
+    at_ref,
+    part0,
+    part3,
+    right_ref,
+    right_far_ref,
+    left_ref,
+    left_far_ref,
+    product_ref,
+    right_far,
+    left,
+    left_far,
+    sems,
+):
+    fetches = [
+        pltpu.make_async_copy(right_far_ref, right_far, sems.at[0]),
+        pltpu.make_async_copy(left_ref, left, sems.at[1]),
+        pltpu.make_async_copy(left_far_ref, left_far, sems.at[2]),
+    ]
+    for fetch in fetches:
+        fetch.start()
+    terms = right_ref.shape[0]
+    for k in range(terms):
+        sector = wanted_ref[k]
+        start = at_ref[0] + 16 - sector
+        multiply((0, 3), (part0, part3), sector, start, right_ref[k], product_ref, k)
+    fetches[0].wait()
+    for k in range(terms):
+        sector = wanted_far_ref[k]
+        start = at_ref[0] + 16 - sector
+        multiply((0, 3), (part0, part3), sector, start, right_far[k], product_ref, terms + k)
+    fetches[1].wait()
+    fetches[2].wait()
+
+
+def late_sum(
+    wanted_ref,
+    wanted_far_ref,
+    at_ref,
+    part1,
+    part2,
+    right_ref,
+    right_far_ref,
+    left_ref,
+    left_far_ref,
+    early_ref,
+    product_ref,
+    keep_ref,
+    send_ref,
 ):
     terms = right_ref.shape[0]
-    rest = [q for q in range(4) if q not in quarters]
-    zeros = jnp.zeros((UNIT, B), jnp.bfloat16)
-
-    def multiply(sector, right, slot):
-        start = at_ref[0] + 16 - sector
-        rows = jnp.concatenate([p[x, sector] for p in parts for x in range(NX)], axis=0)
-        result = jnp.dot(rows, right, preferred_element_type=jnp.float32).astype(jnp.bfloat16)
-        base = slot * (HALF // UNIT)
-        for i, q in enumerate(quarters):
-            for x in range(NX):
-                at = (i * NX + x) * UNIT
-                product[base + x * 4 + ((start + q - 2 * x) & 3)] = result[at : at + UNIT]
-        for q in rest:
-            for x in range(NX):
-                product[base + x * 4 + ((start + q - 2 * x) & 3)] = zeros
-
     for k in range(terms):
-        multiply(wanted_ref[k], right_ref[k], k)
-        multiply(wanted_far_ref[k], right_far_ref[k], terms + k)
+        for sector, right, slot in (
+            (wanted_ref[k], right_ref[k], k),
+            (wanted_far_ref[k], right_far_ref[k], terms + k),
+        ):
+            start = at_ref[0] + 16 - sector
+            multiply((1, 2), (part1, part2), sector, start, right, product_ref, slot)
     middle = terms * HALF // UNIT
-    return jnp.dot(
+    total = jnp.dot(
         left_ref[...],
-        product[:middle].reshape(terms * HALF, B),
+        product_ref[:middle].reshape(terms * HALF, B),
         preferred_element_type=jnp.float32,
     ) + jnp.dot(
         left_far_ref[...],
-        product[middle:].reshape(terms * HALF, B),
+        product_ref[middle:].reshape(terms * HALF, B),
         preferred_element_type=jnp.float32,
     )
-
-
-def early_sum(
-    wanted_ref, wanted_far_ref, at_ref, part0, part3, right_ref, right_far_ref, left_ref, left_far_ref, total_ref, product
-):
-    total_ref[...] = partial_sum(
-        (0, 3), wanted_ref, wanted_far_ref, at_ref, (part0, part3), right_ref, right_far_ref, left_ref, left_far_ref, product
-    )
-
-
-def late_sum(
-    wanted_ref, wanted_far_ref, at_ref, part1, part2, right_ref, right_far_ref, left_ref, left_far_ref, early_ref, keep_ref, send_ref, product
-):
-    total = early_ref[...] + partial_sum(
-        (1, 2), wanted_ref, wanted_far_ref, at_ref, (part1, part2), right_ref, right_far_ref, left_ref, left_far_ref, product
-    )
+    row = lax.broadcasted_iota(jnp.int32, (B, B), 0)
+    col = lax.broadcasted_iota(jnp.int32, (B, B), 1)
+    total = jnp.where((row < at_ref[2]) & (col < at_ref[2]), total, 0.0)
     pairs = total.reshape(NX * NY, 2, ROWS, B)
     low, high = pairs[:, 0], pairs[:, 1]
     first = at_ref[1] == 0
@@ -126,10 +160,14 @@
     right = right_ops.reshape(term_count, B, B)
     wanted = source.reshape(term_count)
 
-    own_rows = ((x * NY + y) * NC + c) * ROWS + jnp.arange(ROWS, dtype=jnp.int32)
-    columns = jnp.arange(B, dtype=jnp.int32)
-    inside = (own_rows[:, None] < sizes[0]) & (columns[None, :] < sizes[0])
-    masked = jnp.where(inside, psi[0], jnp.zeros((), psi.dtype))
+    shape = (2 * NZ, ROWS, B)
+    row = ((x * NY + y) * NC + c) * ROWS + lax.broadcasted_iota(jnp.int32, shape, 1)
+    col = lax.broadcasted_iota(jnp.int32, shape, 2)
+    masked = jnp.where(
+        (row < sizes[0]) & (col < sizes[0]),
+        jnp.broadcast_to(psi, shape),
+        jnp.zeros((), psi.dtype),
+    )
 
     core = c.astype(jnp.int32).reshape(1)
     left_own, left_other = pl.pallas_call(
@@ -147,7 +185,7 @@
     wanted_far = lax.ppermute(wanted, "c", swap)
 
     far = lax.all_to_all(
-        jnp.broadcast_to(masked[None], (2 * NZ, ROWS, B)),
+        masked,
         ("y", "z"),
         0,
         0,
@@ -172,8 +210,8 @@
 
     in_smem = pl.BlockSpec(memory_space=pltpu.SMEM)
     in_vmem = pl.BlockSpec(memory_space=pltpu.VMEM)
+    in_any = pl.BlockSpec(memory_space=pl.ANY)
     settings = dict(
-        scratch_shapes=[pltpu.VMEM((2 * term_count * HALF // UNIT, UNIT, B), jnp.bfloat16)],
         compiler_params=pltpu.CompilerParams(vmem_limit_bytes=16 * 1024 * 1024),
         cost_estimate=pl.CostEstimate(
             flops=4 * term_count * HALF * B * B,
@@ -181,28 +219,37 @@
             transcendentals=0,
         ),
     )
-    at = jnp.stack([(2 * x + y + z).astype(jnp.int32), c.astype(jnp.int32)])
-    early = pl.pallas_call(
-        early_sum,
-        in_specs=[in_smem] * 3 + [in_vmem] * 6,
-        out_specs=in_vmem,
-        out_shape=jax.ShapeDtypeStruct((B, B), jnp.float32),
+    at = jnp.stack([(2 * x + y + z).astype(jnp.int32), c.astype(jnp.int32), sizes[0]])
+    product_shape = jax.ShapeDtypeStruct((2 * term_count * HALF // UNIT, UNIT, B), jnp.bfloat16)
+    left_shape = jax.ShapeDtypeStruct((B, term_count * HALF), jnp.bfloat16)
+    early, right_far, left_own, left_far = pl.pallas_call(
+        early_products,
+        in_specs=[in_smem] * 3 + [in_vmem] * 3 + [in_any] * 3,
+        out_specs=[in_vmem] * 4,
+        out_shape=[
+            product_shape,
+            jax.ShapeDtypeStruct((term_count, B, B), jnp.bfloat16),
+            left_shape,
+            left_shape,
+        ],
+        scratch_shapes=[pltpu.SemaphoreType.DMA((3,))],
         **settings,
     )(wanted, wanted_far, at, part, down, right, right_far, left_own, left_far)
-    keep, send = pl.pallas_call(
+    _, keep, send = pl.pallas_call(
         late_sum,
         in_specs=[in_smem] * 3 + [in_vmem] * 7,
-        out_specs=[in_vmem] * 2,
+        out_specs=[in_vmem] * 3,
         out_shape=[
+            product_shape,
             jax.ShapeDtypeStruct((NX * NY, ROWS, B), jnp.float32),
             jax.ShapeDtypeStruct((NX * NY, ROWS, B), jnp.bfloat16),
         ],
+        input_output_aliases={9: 0},
         **settings,
     )(wanted, wanted_far, at, up, across, right, right_far, left_own, left_far, early)
     chip_sum = keep + lax.ppermute(send, "c", swap).astype(jnp.float32)
     shares = lax.all_to_all(chip_sum.astype(jnp.bfloat16), CHIP, 0, 0, tiled=True)
-    summed = jnp.sum(shares.astype(jnp.float32), axis=0)
-    return jnp.where(inside, summed, jnp.float32(0.0)).astype(jnp.bfloat16)[:, None, :]
+    return jnp.sum(shares[:, :, None, :].astype(jnp.float32), axis=0).astype(jnp.bfloat16)
 
 
 def solution(mesh):

time: 108 us -> 107 us (level)
  Pallas kernels: 12.6 us -> 11.1 us
    select_n x0 -> x1, other arithmetic: none -> 1.47 us  [on_device(): jnp.where((row < sizes[0]) & (col < sizes[0]), jnp.broadcast_to(psi, shap...]
    ppermute x1, waiting for transfers between devices: 2.19 us -> 3.43 us  [on_device(): across = lax.ppermute(part, ALL, shifts((1, 0, 0), (-1, 0, 0)))]
  transfers between devices with their start and end apart: 9 -> 9, of which waited for: 5 -> 5; matrix products, arithmetic and copies ran while one was open for 0% -> 0% of each run, Pallas kernels for 8% -> 7%
where the time goes in v3:
time: 107 us
  starting transfers between devices  43.1 us (40%)
  waiting for transfers between devices  25 us (23%)
  blocking collectives  22.1 us (21%)
  Pallas kernels  11.1 us (10%)
  other arithmetic  2.28 us (2%)
  local copies, waits for them, and re-layouts  2.25 us (2%)
    all_to_all x1, blocking collectives, on_device(): lax.all_to_all(chip_sum.astype(jnp.bfloat16), CHIP, 0, 0, tiled=True)  22.1 us
    all_to_all x1, starting transfers between devices, on_device(): lax.all_to_all(masked, ('y', 'z'), 0, 0, axis_index_groups=far_groups(),...  18.9 us
    all_to_all x1, waiting for transfers between devices, on_device(): lax.all_to_all(masked, ('y', 'z'), 0, 0, axis_index_groups=far_groups(),...  11 us
    all_to_all x1, waiting for transfers between devices, on_device(): lax.all_to_all(jnp.broadcast_to(far[None], (NX, NZ, UNIT, B)), ('x', 'y',...  6.89 us
    ppermute x1, starting transfers between devices, on_device(): across = lax.ppermute(part, ALL, shifts((1, 0, 0), (-1, 0, 0)))  5.83 us
    pallas_call x1, Pallas kernels, on_device(): pl.pallas_call(split_columns, grid_spec=pltpu.PrefetchScalarGridSpec(num_...  4.68 us
    all_to_all x1, starting transfers between devices, on_device(): lax.all_to_all(jnp.broadcast_to(far[None], (NX, NZ, UNIT, B)), ('x', 'y',...  4.29 us
    ppermute x1, starting transfers between devices, on_device(): up = lax.ppermute(part, ALL, shifts((0, 1, 0), (0, 0, 1)))  3.93 us
  transfers between devices with their start and end apart: 9, of which 5 were waited for; matrix products, arithmetic and copies ran while one was open for 0% of the time, Pallas kernels for 7%

profile of v3, /device:TPU:8, one launch (start us, length us, event | category | flops | bytes accessed | tf_op | source)
XLA Modules:
  0.0 106.6 jit_solution(3012391922053668403)
XLA Ops:
  0.7 1.5 %and_select_fusion = bf16[24,8,512]{2,1,0:T(8,128)(2,1)} fusion(pred[512]{0:T(512)(128)(4,1)S(1)} %iota_compare_fusion, pred[8]{0:T(512)(128)(4,1)S(1)} %add_compare_fusion, bf16[8,512]{1,0:T(8,128)(2,1)} %bitcast.18), kind=kLoop, calls=%fused_computation.1 | loop fusion | flops 196608 | bytes 205320 | tf_op jit(solution)/shard_map/jit(_where)/select_n | solution.py:166
  2.2 18.9 %all-to-all-start = ((bf16[24,8,512]{2,1,0:T(8,128)(2,1)}), bf16[24,8,512]{2,1,0:T(8,128)(2,1)S(1)}, u32[]{:S(2)}, u32[]{:S(2)}) async-start(bf16[24,8,512]{2,1,0:T(8,128)(2,1)} %and_select_fusion), calls=%async_computation | async-start | bytes 393216 | tf_op jit(solution)/shard_map/all_to_all | solution.py:187
  21.1 1.9 %collective-permute-start = (s32[4]{0:T(128)}, s32[4]{0:T(128)S(1)}, u32[]{:S(2)}, u32[]{:S(2)}) collective-permute-start(s32[4]{0:T(128)} %bitcast.14), channel_id=1, source_target_pairs={{0,12},{12,0},{1,13},{13,1},{2,14},{14,2},{3,15},{15,3},{4,16},{16... | collective-permute-start | bytes 56 | tf_op jit(solution)/shard_map/ppermute | solution.py:185
  23.0 4.7 %shard_map.55 = (bf16[512,1024]{1,0:T(8,128)(2,1)}, bf16[512,1024]{1,0:T(8,128)(2,1)}) custom-call(s32[1]{0:T(128)} %bitcast.4.core_ref, bf16[4,512,512]{2,1,0:T(8,128)(2,1)} %bitcast.19), custom_call_target="tpu_custom_call" | custom-call | flops 1073741824 | bytes 4194304 | tf_op jit(solution)/shard_map/pallas_call | solution.py:173
  27.7 0.0 copy-start
  27.7 0.0 copy-start.2
  27.7 0.0 collective-permute-done.wanted_far_ref
  27.7 11.0 %all-to-all-done = bf16[24,8,512]{2,1,0:T(8,128)(2,1)S(1)} async-done(((bf16[24,8,512]{2,1,0:T(8,128)(2,1)}), bf16[24,8,512]{2,1,0:T(8,128)(2,1)S(1)}, u32[]{:S(2)}, u32[]{:S(2)}) %all-to-all-start) | async-done | bytes 196640 | tf_op jit(solution)/shard_map/all_to_all | solution.py:187
  38.7 1.0 broadcast_in_dim.21
  39.7 4.3 %all-to-all-start.1 = ((bf16[4,12,16,512]{3,2,1,0:T(8,128)(2,1)}), bf16[4,12,16,512]{3,2,1,0:T(8,128)(2,1)S(1)}, u32[]{:S(2)}, u32[]{:S(2)}) async-start(bf16[4,12,16,512]{3,2,1,0:T(8,128)(2,1)} %broadcast_in_dim.21), calls=%async_computation.1 | async-start | bytes 1572864 | tf_op jit(solution)/shard_map/all_to_all | solution.py:199
  44.0 0.0 copy-done
  44.0 1.9 %collective-permute-start.4 = (bf16[4,512,512]{2,1,0:T(8,128)(2,1)S(1)}, bf16[4,512,512]{2,1,0:T(8,128)(2,1)}, u32[]{:S(2)}, u32[]{:S(2)}) collective-permute-start(bf16[4,512,512]{2,1,0:T(8,128)(2,1)S(1)} %bitcast.11), channel_id=1, source_target_pairs={{0,12},{12,0},{1,13},{13,1},{2,14},{14,2},{3,15},{15,3},{4,16},{16... | collective-permute-start | bytes 6291464 | tf_op jit(solution)/shard_map/ppermute | solution.py:184
  45.9 2.4 %collective-permute-start.5 = (bf16[512,1024]{1,0:T(8,128)(2,1)}, bf16[512,1024]{1,0:T(8,128)(2,1)}, u32[]{:S(2)}, u32[]{:S(2)}) collective-permute-start(bf16[512,1024]{1,0:T(8,128)(2,1)} %get-tuple-element.22), channel_id=1, source_target_pairs={{0,12},{12,0},{1,13},{13,1},{2,14},{14,2},{3,15},{15,3},{4,16},{16... | collective-permute-start | bytes 3145736 | tf_op jit(solution)/shard_map/ppermute | solution.py:198
  48.3 6.9 %all-to-all-done.1.part0 = bf16[4,12,16,512]{3,2,1,0:T(8,128)(2,1)S(1)} async-done(((bf16[4,12,16,512]{3,2,1,0:T(8,128)(2,1)}), bf16[4,12,16,512]{3,2,1,0:T(8,128)(2,1)S(1)}, u32[]{:S(2)}, u32[]{:S(2)}) %all-to-all-start.1) | async-done | bytes 786464 | tf_op jit(solution)/shard_map/all_to_all | solution.py:199
  55.2 1.9 %collective-permute-start.3 = (bf16[4,12,16,512]{3,2,1,0:T(8,128)(2,1)S(1)}, bf16[4,12,16,512]{3,2,1,0:T(8,128)(2,1)}, u32[]{:S(2)}, u32[]{:S(2)}) collective-permute-start(bf16[4,12,16,512]{3,2,1,0:T(8,128)(2,1)S(1)} %all-to-all-done.1.part0), channel_id=1, source_target_pairs={{168,0},{169,1},{170,2},{171,3},{172,4},{173,5},{174,6},{175,7},{1... | collective-permute-start | bytes 2359304 | tf_op jit(solution)/shard_map/ppermute | solution.py:208
  57.1 3.9 %collective-permute-start.1 = (bf16[4,12,16,512]{3,2,1,0:T(8,128)(2,1)S(1)}, bf16[4,12,16,512]{3,2,1,0:T(8,128)(2,1)}, u32[]{:S(2)}, u32[]{:S(2)}) collective-permute-start(bf16[4,12,16,512]{3,2,1,0:T(8,128)(2,1)S(1)} %all-to-all-done.1.part0), channel_id=1, source_target_pairs={{24,0},{25,1},{26,2},{27,3},{28,4},{29,5},{30,6},{31,7},{32,8},{33... | collective-permute-start | bytes 2359304 | tf_op jit(solution)/shard_map/ppermute | solution.py:207
  61.1 5.8 %collective-permute-start.2 = (bf16[4,12,16,512]{3,2,1,0:T(8,128)(2,1)S(1)}, bf16[4,12,16,512]{3,2,1,0:T(8,128)(2,1)}, u32[]{:S(2)}, u32[]{:S(2)}) collective-permute-start(bf16[4,12,16,512]{3,2,1,0:T(8,128)(2,1)S(1)} %all-to-all-done.1.part0), channel_id=1, source_target_pairs={{192,0},{193,1},{194,2},{195,3},{196,4},{197,5},{198,6},{199,7},{2... | collective-permute-start | bytes 2359304 | tf_op jit(solution)/shard_map/ppermute | solution.py:209
  66.9 0.1 pad_add_fusion.at_ref
  67.0 0.0 collective-permute-done.5.left_far_ref
  67.0 0.0 collective-permute-done.4.right_far_ref
  67.0 2.2 %collective-permute-done.3.part3 = bf16[4,12,16,512]{3,2,1,0:T(8,128)(2,1)} collective-permute-done((bf16[4,12,16,512]{3,2,1,0:T(8,128)(2,1)S(1)}, bf16[4,12,16,512]{3,2,1,0:T(8,128)(2,1)}, u32[]{:S(2)}, u32[]{:S(2)}) %collective-permute-start.3) | collective-permute-done | bytes 786464 | tf_op jit(solution)/shard_map/ppermute | solution.py:208
  69.2 0.0 copy-done.2
  69.2 0.0 copy-start.1
  69.2 1.2 %copy-done.1 = bf16[512,1024]{1,0:T(8,128)(2,1)S(1)} copy-done((bf16[512,1024]{1,0:T(8,128)(2,1)S(1)}, bf16[512,1024]{1,0:T(8,128)(2,1)}, u32[]{:S(2)}) %copy-start.1) | copy-done | bytes 1048600
  70.4 3.2 %shard_map.56 = (bf16[128,16,512]{2,1,0:T(8,128)(2,1)S(1)}, bf16[4,512,512]{2,1,0:T(8,128)(2,1)S(1)}, bf16[512,1024]{1,0:T(8,128)(2,1)S(1)}, bf16[512,1024]{1,0:T(8,128)(2,1)S(1)}) custom-call(s32[4]{0:T(128)S(1)} %bitcast.15, s32[4]{0:T(128)S(1)} %collective-permute-done.wanted_far_ref, s32[3]{0:T(128)S(1)} %pad_add_fusion.at_ref, ...), custom_call_target="tpu_custom_call" | custom-call | flops 1073741824 | bytes 8388608 | tf_op jit(solution)/shard_map/pallas_call | solution.py:225
  73.7 0.0 collective-permute-done.1.part1
  73.7 3.4 %collective-permute-done.2.part2 = bf16[4,12,16,512]{3,2,1,0:T(8,128)(2,1)} collective-permute-done((bf16[4,12,16,512]{3,2,1,0:T(8,128)(2,1)S(1)}, bf16[4,12,16,512]{3,2,1,0:T(8,128)(2,1)}, u32[]{:S(2)}, u32[]{:S(2)}) %collective-permute-start.2) | collective-permute-done | bytes 786464 | tf_op jit(solution)/shard_map/ppermute | solution.py:209
  77.1 3.2 %shard_map.57 = (bf16[128,16,512]{2,1,0:T(8,128)(2,1)S(1)}, f32[32,8,512]{2,1,0:T(8,128)S(1)}, bf16[32,8,512]{2,1,0:T(8,128)(2,1)S(1)}) custom-call(s32[4]{0:T(128)S(1)} %bitcast.16, s32[4]{0:T(128)S(1)} %collective-permute-done.wanted_far_ref, s32[3]{0:T(128)S(1)} %pad_add_fusion.at_ref, ...), custom_call_target="tpu_custom_call", output_to_operand_aliasing={{0}: (9, {})} | custom-call | flops 1073741824 | bytes 8388608 | tf_op jit(solution)/shard_map/pallas_call | solution.py:238
  80.3 1.9 %collective-permute-start.6 = (bf16[32,8,512]{2,1,0:T(8,128)(2,1)S(1)}, bf16[32,8,512]{2,1,0:T(8,128)(2,1)S(1)}, u32[]{:S(2)}, u32[]{:S(2)}) collective-permute-start(bf16[32,8,512]{2,1,0:T(8,128)(2,1)S(1)} %get-tuple-element.28), channel_id=1, source_target_pairs={{0,12},{12,0},{1,13},{13,1},{2,14},{14,2},{3,15},{15,3},{4,16},{16... | collective-permute-start | bytes 786440 | tf_op jit(solution)/shard_map/ppermute | solution.py:250
  82.2 1.5 %collective-permute-done.6 = bf16[32,8,512]{2,1,0:T(8,128)(2,1)S(1)} collective-permute-done((bf16[32,8,512]{2,1,0:T(8,128)(2,1)S(1)}, bf16[32,8,512]{2,1,0:T(8,128)(2,1)S(1)}, u32[]{:S(2)}, u32[]{:S(2)}) %collective-permute-start.6) | collective-permute-done | bytes 262176 | tf_op jit(solution)/shard_map/ppermute | solution.py:250
  83.7 0.1 add_convert_fusion
  83.8 22.1 %all_to_all.15 = bf16[32,8,512]{2,1,0:T(8,128)(2,1)S(1)} all-to-all(bf16[32,8,512]{2,1,0:T(8,128)(2,1)S(1)} %add_convert_fusion), channel_id=1, replica_groups=mesh['x'=4,'y'=8,'c'=2,'z'=12] {'x','y'}, dimensions={0} | all-to-all | bytes 524288 | tf_op jit(solution)/shard_map/all_to_all | solution.py:251
  105.9 0.6 reduce_sum.14
  (2 shorter events, 0.0 us)
Async XLA Ops:
  2.2 36.5 %all-to-all-start = ((bf16[24,8,512]{2,1,0:T(8,128)(2,1)}), bf16[24,8,512]{2,1,0:T(8,128)(2,1)S(1)}, u32[]{:S(2)}, u32[]{:S(2)}) async-start(bf16[24,8,512]{2,1,0:T(8,128)(2,1)} %and_select_fusion), calls=%async_computation | async-start | bytes 393216 | tf_op jit(solution)/shard_map/all_to_all | solution.py:187
  21.1 6.6 %collective-permute-start = (s32[4]{0:T(128)}, s32[4]{0:T(128)S(1)}, u32[]{:S(2)}, u32[]{:S(2)}) collective-permute-start(s32[4]{0:T(128)} %bitcast.14), channel_id=1, source_target_pairs={{0,12},{12,0},{1,13},{13,1},{2,14},{14,2},{3,15},{15,3},{4,16},{16... | collective-permute-start | bytes 56 | tf_op jit(solution)/shard_map/ppermute | solution.py:185
  27.7 16.3 %copy-start = (bf16[4,1,512,512]{3,2,1,0:T(8,128)(2,1)S(1)}, bf16[4,1,512,512]{3,2,1,0:T(8,128)(2,1)}, u32[]{:S(2)}) copy-start(bf16[4,1,512,512]{3,2,1,0:T(8,128)(2,1)} %param.8) | copy-start | bytes 6291460
  27.7 41.5 %copy-start.2 = (s32[4,1]{0,1:T(1,128)S(1)}, s32[4,1]{0,1:T(1,128)}, u32[]{:S(2)}) copy-start(s32[4,1]{0,1:T(1,128)} %param.9) | copy-start | bytes 52
  39.7 15.5 %all-to-all-start.1 = ((bf16[4,12,16,512]{3,2,1,0:T(8,128)(2,1)}), bf16[4,12,16,512]{3,2,1,0:T(8,128)(2,1)S(1)}, u32[]{:S(2)}, u32[]{:S(2)}) async-start(bf16[4,12,16,512]{3,2,1,0:T(8,128)(2,1)} %broadcast_in_dim.21), calls=%async_computation.1 | async-start | bytes 1572864 | tf_op jit(solution)/shard_map/all_to_all | solution.py:199
  44.0 23.0 %collective-permute-start.4 = (bf16[4,512,512]{2,1,0:T(8,128)(2,1)S(1)}, bf16[4,512,512]{2,1,0:T(8,128)(2,1)}, u32[]{:S(2)}, u32[]{:S(2)}) collective-permute-start(bf16[4,512,512]{2,1,0:T(8,128)(2,1)S(1)} %bitcast.11), channel_id=1, source_target_pairs={{0,12},{12,0},{1,13},{13,1},{2,14},{14,2},{3,15},{15,3},{4,16},{16... | collective-permute-start | bytes 6291464 | tf_op jit(solution)/shard_map/ppermute | solution.py:184
  45.9 21.1 %collective-permute-start.5 = (bf16[512,1024]{1,0:T(8,128)(2,1)}, bf16[512,1024]{1,0:T(8,128)(2,1)}, u32[]{:S(2)}, u32[]{:S(2)}) collective-permute-start(bf16[512,1024]{1,0:T(8,128)(2,1)} %get-tuple-element.22), channel_id=1, source_target_pairs={{0,12},{12,0},{1,13},{13,1},{2,14},{14,2},{3,15},{15,3},{4,16},{16... | collective-permute-start | bytes 3145736 | tf_op jit(solution)/shard_map/ppermute | solution.py:198
  55.2 14.0 %collective-permute-start.3 = (bf16[4,12,16,512]{3,2,1,0:T(8,128)(2,1)S(1)}, bf16[4,12,16,512]{3,2,1,0:T(8,128)(2,1)}, u32[]{:S(2)}, u32[]{:S(2)}) collective-permute-start(bf16[4,12,16,512]{3,2,1,0:T(8,128)(2,1)S(1)} %all-to-all-done.1.part0), channel_id=1, source_target_pairs={{168,0},{169,1},{170,2},{171,3},{172,4},{173,5},{174,6},{175,7},{1... | collective-permute-start | bytes 2359304 | tf_op jit(solution)/shard_map/ppermute | solution.py:208
  57.1 16.5 %collective-permute-start.1 = (bf16[4,12,16,512]{3,2,1,0:T(8,128)(2,1)S(1)}, bf16[4,12,16,512]{3,2,1,0:T(8,128)(2,1)}, u32[]{:S(2)}, u32[]{:S(2)}) collective-permute-start(bf16[4,12,16,512]{3,2,1,0:T(8,128)(2,1)S(1)} %all-to-all-done.1.part0), channel_id=1, source_target_pairs={{24,0},{25,1},{26,2},{27,3},{28,4},{29,5},{30,6},{31,7},{32,8},{33... | collective-permute-start | bytes 2359304 | tf_op jit(solution)/shard_map/ppermute | solution.py:207
  61.1 16.0 %collective-permute-start.2 = (bf16[4,12,16,512]{3,2,1,0:T(8,128)(2,1)S(1)}, bf16[4,12,16,512]{3,2,1,0:T(8,128)(2,1)}, u32[]{:S(2)}, u32[]{:S(2)}) collective-permute-start(bf16[4,12,16,512]{3,2,1,0:T(8,128)(2,1)S(1)} %all-to-all-done.1.part0), channel_id=1, source_target_pairs={{192,0},{193,1},{194,2},{195,3},{196,4},{197,5},{198,6},{199,7},{2... | collective-permute-start | bytes 2359304 | tf_op jit(solution)/shard_map/ppermute | solution.py:209
  69.2 1.2 %copy-start.1 = (bf16[512,1024]{1,0:T(8,128)(2,1)S(1)}, bf16[512,1024]{1,0:T(8,128)(2,1)}, u32[]{:S(2)}) copy-start(bf16[512,1024]{1,0:T(8,128)(2,1)} %get-tuple-element.21.left_ref) | copy-start | bytes 3145732
  80.3 3.4 %collective-permute-start.6 = (bf16[32,8,512]{2,1,0:T(8,128)(2,1)S(1)}, bf16[32,8,512]{2,1,0:T(8,128)(2,1)S(1)}, u32[]{:S(2)}, u32[]{:S(2)}) collective-permute-start(bf16[32,8,512]{2,1,0:T(8,128)(2,1)S(1)} %get-tuple-element.28), channel_id=1, source_target_pairs={{0,12},{12,0},{1,13},{13,1},{2,14},{14,2},{3,15},{15,3},{4,16},{16... | collective-permute-start | bytes 786440 | tf_op jit(solution)/shard_map/ppermute | solution.py:250

commit v4 on v3

--- a/solution.py
+++ b/solution.py
@@ -46,20 +46,21 @@
 
 
 def split_columns(core_ref, left_ref, own_ref, other_ref):
-    core = core_ref[0]
     row = lax.broadcasted_iota(jnp.int32, (B, B), 0)
-    col = lax.broadcasted_iota(jnp.int32, (B, B), 1)
+    col = lax.broadcasted_iota(jnp.int32, (1, B), 1)
     where_from = (
         ((col >> 6) & 3) * 128
         + ((col >> 3) & 1) * 64
         + ((col >> 4) & 3) * 16
-        + (((col >> 8) & 1) ^ core) * 8
+        + (((col >> 8) & 1) ^ core_ref[0]) * 8
         + (col & 7)
     )
     pick = jnp.where(row == where_from, 1.0, 0.0).astype(jnp.bfloat16)
-    moved = jnp.dot(left_ref[0], pick, preferred_element_type=jnp.float32).astype(jnp.bfloat16)
-    own_ref[...] = moved[:, :HALF]
-    other_ref[...] = moved[:, HALF:]
+    for k in range(left_ref.shape[0]):
+        moved = jnp.dot(left_ref[k], pick, preferred_element_type=jnp.float32).astype(jnp.bfloat16)
+        columns = slice(k * HALF, k * HALF + HALF)
+        own_ref[:, columns] = moved[:, :HALF]
+        other_ref[:, columns] = moved[:, HALF:]
 
 
 def multiply(quarters, parts, sector, start, right, product, slot):
@@ -172,13 +173,10 @@
     core = c.astype(jnp.int32).reshape(1)
     left_own, left_other = pl.pallas_call(
         split_columns,
-        grid_spec=pltpu.PrefetchScalarGridSpec(
-            num_scalar_prefetch=1,
-            grid=(term_count,),
-            in_specs=[pl.BlockSpec((1, B, B), lambda k, core: (k, 0, 0))],
-            out_specs=[pl.BlockSpec((B, HALF), lambda k, core: (0, k))] * 2,
-        ),
+        in_specs=[pl.BlockSpec(memory_space=pltpu.SMEM), pl.BlockSpec(memory_space=pltpu.VMEM)],
+        out_specs=[pl.BlockSpec(memory_space=pltpu.VMEM)] * 2,
         out_shape=[jax.ShapeDtypeStruct((B, term_count * HALF), jnp.bfloat16)] * 2,
+        compiler_params=pltpu.CompilerParams(vmem_limit_bytes=48 * 1024 * 1024),
         cost_estimate=pl.CostEstimate(flops=2 * term_count * B**3, bytes_accessed=4 * term_count * B * B, transcendentals=0),
     )(core, left)
     right_far = lax.ppermute(right, "c", swap)
@@ -212,7 +210,7 @@
     in_vmem = pl.BlockSpec(memory_space=pltpu.VMEM)
     in_any = pl.BlockSpec(memory_space=pl.ANY)
     settings = dict(
-        compiler_params=pltpu.CompilerParams(vmem_limit_bytes=16 * 1024 * 1024),
+        compiler_params=pltpu.CompilerParams(vmem_limit_bytes=9 * 1024 * 1024),
         cost_estimate=pl.CostEstimate(
             flops=4 * term_count * HALF * B * B,
             bytes_accessed=16 * term_count * HALF * B,

time: 107 us -> 107 us (level)
  local copies, waits for them, and re-layouts: 2.25 us -> 5.8 us
  Pallas kernels: 11.1 us -> 7.7 us
    unnamed x6 -> x12, local copies, waits for them, and re-layouts: 1.23 us -> 4.78 us
    pallas_call x1, Pallas kernels: 4.68 us -> 1.27 us  [on_device(): pl.pallas_call(split_columns, in_specs=[pl.BlockSpec(memory_space=pltpu.S...]
  transfers between devices with their start and end apart: 9 -> 9, of which waited for: 5 -> 5; matrix products, arithmetic and copies ran while one was open for 0% -> 0% of each run, Pallas kernels for 7% -> 4%
where the time goes in v4:
time: 107 us
  starting transfers between devices  43.1 us (40%)
  waiting for transfers between devices  24.8 us (23%)
  blocking collectives  22.1 us (21%)
  Pallas kernels  7.7 us (7%)
  local copies, waits for them, and re-layouts  5.8 us (5%)
  other arithmetic  2.28 us (2%)
    all_to_all x1, blocking collectives, on_device(): lax.all_to_all(chip_sum.astype(jnp.bfloat16), CHIP, 0, 0, tiled=True)  22.1 us
    all_to_all x1, starting transfers between devices, on_device(): lax.all_to_all(masked, ('y', 'z'), 0, 0, axis_index_groups=far_groups(),...  18.9 us
    all_to_all x1, waiting for transfers between devices, on_device(): lax.all_to_all(masked, ('y', 'z'), 0, 0, axis_index_groups=far_groups(),...  10.8 us
    all_to_all x1, waiting for transfers between devices, on_device(): lax.all_to_all(jnp.broadcast_to(far[None], (NX, NZ, UNIT, B)), ('x', 'y',...  6.89 us
    ppermute x1, starting transfers between devices, on_device(): across = lax.ppermute(part, ALL, shifts((1, 0, 0), (-1, 0, 0)))  5.83 us
    unnamed x12, local copies, waits for them, and re-layouts  4.78 us
    all_to_all x1, starting transfers between devices, on_device(): lax.all_to_all(jnp.broadcast_to(far[None], (NX, NZ, UNIT, B)), ('x', 'y',...  4.29 us
    ppermute x1, starting transfers between devices, on_device(): up = lax.ppermute(part, ALL, shifts((0, 1, 0), (0, 0, 1)))  3.93 us
  transfers between devices with their start and end apart: 9, of which 5 were waited for; matrix products, arithmetic and copies ran while one was open for 0% of the time, Pallas kernels for 4%

profile of v4, /device:TPU:8, one launch (start us, length us, event | category | flops | bytes accessed | tf_op | source)
XLA Modules:
  0.0 106.5 jit_solution(12554897919707775916)
XLA Ops:
  0.7 1.5 %and_select_fusion = bf16[24,8,512]{2,1,0:T(8,128)(2,1)} fusion(pred[512]{0:T(512)(128)(4,1)S(1)} %iota_compare_fusion, pred[8]{0:T(512)(128)(4,1)S(1)} %add_compare_fusion, bf16[8,512]{1,0:T(8,128)(2,1)} %bitcast.19), kind=kLoop, calls=%fused_computation.1 | loop fusion | flops 196608 | bytes 205320 | tf_op jit(solution)/shard_map/jit(_where)/select_n | solution.py:167
  2.1 18.9 %all-to-all-start = ((bf16[24,8,512]{2,1,0:T(8,128)(2,1)}), bf16[24,8,512]{2,1,0:T(8,128)(2,1)S(1)}, u32[]{:S(2)}, u32[]{:S(2)}) async-start(bf16[24,8,512]{2,1,0:T(8,128)(2,1)} %and_select_fusion), calls=%async_computation | async-start | bytes 393216 | tf_op jit(solution)/shard_map/all_to_all | solution.py:185
  21.1 1.9 %collective-permute-start = (s32[4]{0:T(128)}, s32[4]{0:T(128)S(1)}, u32[]{:S(2)}, u32[]{:S(2)}) collective-permute-start(s32[4]{0:T(128)} %bitcast.14), channel_id=1, source_target_pairs={{0,12},{12,0},{1,13},{13,1},{2,14},{14,2},{3,15},{15,3},{4,16},{16... | collective-permute-start | bytes 56 | tf_op jit(solution)/shard_map/ppermute | solution.py:183
  23.0 0.0 copy-start.4
  23.0 1.6 %copy-done.4 = bf16[4,1,512,512]{3,2,1,0:T(8,128)(2,1)S(1)} copy-done((bf16[4,1,512,512]{3,2,1,0:T(8,128)(2,1)S(1)}, bf16[4,1,512,512]{3,2,1,0:T(8,128)(2,1)}, u32[]{:S(2)}) %copy-start.4) | copy-done | bytes 2097176
  24.6 1.3 %shard_map.55 = (bf16[512,1024]{1,0:T(8,128)(2,1)S(1)}, bf16[512,1024]{1,0:T(8,128)(2,1)S(1)}) custom-call(s32[1]{0:T(128)} %bitcast.4.core_ref, bf16[4,512,512]{2,1,0:T(8,128)(2,1)S(1)} %bitcast.17), custom_call_target="tpu_custom_call" | custom-call | flops 1073741824 | bytes 4194304 | tf_op jit(solution)/shard_map/pallas_call | solution.py:174
  25.9 0.0 copy-start.1
  25.9 1.0 copy-done.1
  26.9 0.0 copy-start.5
  26.9 1.0 copy-done.5
  27.9 0.0 copy-start
  27.9 0.0 copy-start.3
  27.9 0.0 collective-permute-done.wanted_far_ref
  27.9 10.8 %all-to-all-done = bf16[24,8,512]{2,1,0:T(8,128)(2,1)S(1)} async-done(((bf16[24,8,512]{2,1,0:T(8,128)(2,1)}), bf16[24,8,512]{2,1,0:T(8,128)(2,1)S(1)}, u32[]{:S(2)}, u32[]{:S(2)}) %all-to-all-start) | async-done | bytes 196640 | tf_op jit(solution)/shard_map/all_to_all | solution.py:185
  38.7 1.0 broadcast_in_dim.21
  39.7 4.3 %all-to-all-start.1 = ((bf16[4,12,16,512]{3,2,1,0:T(8,128)(2,1)}), bf16[4,12,16,512]{3,2,1,0:T(8,128)(2,1)S(1)}, u32[]{:S(2)}, u32[]{:S(2)}) async-start(bf16[4,12,16,512]{3,2,1,0:T(8,128)(2,1)} %broadcast_in_dim.21), calls=%async_computation.1 | async-start | bytes 1572864 | tf_op jit(solution)/shard_map/all_to_all | solution.py:197
  44.0 0.0 copy-done
  44.0 1.9 %collective-permute-start.4 = (bf16[4,512,512]{2,1,0:T(8,128)(2,1)S(1)}, bf16[4,512,512]{2,1,0:T(8,128)(2,1)}, u32[]{:S(2)}, u32[]{:S(2)}) collective-permute-start(bf16[4,512,512]{2,1,0:T(8,128)(2,1)S(1)} %bitcast.11), channel_id=1, source_target_pairs={{0,12},{12,0},{1,13},{13,1},{2,14},{14,2},{3,15},{15,3},{4,16},{16... | collective-permute-start | bytes 6291464 | tf_op jit(solution)/shard_map/ppermute | solution.py:182
  45.9 2.4 %collective-permute-start.5 = (bf16[512,1024]{1,0:T(8,128)(2,1)}, bf16[512,1024]{1,0:T(8,128)(2,1)}, u32[]{:S(2)}, u32[]{:S(2)}) collective-permute-start(bf16[512,1024]{1,0:T(8,128)(2,1)} %copy-done.5), channel_id=1, source_target_pairs={{0,12},{12,0},{1,13},{13,1},{2,14},{14,2},{3,15},{15,3},{4,16},{16... | collective-permute-start | bytes 3145736 | tf_op jit(solution)/shard_map/ppermute | solution.py:196
  48.3 6.9 %all-to-all-done.1.part0 = bf16[4,12,16,512]{3,2,1,0:T(8,128)(2,1)S(1)} async-done(((bf16[4,12,16,512]{3,2,1,0:T(8,128)(2,1)}), bf16[4,12,16,512]{3,2,1,0:T(8,128)(2,1)S(1)}, u32[]{:S(2)}, u32[]{:S(2)}) %all-to-all-start.1) | async-done | bytes 786464 | tf_op jit(solution)/shard_map/all_to_all | solution.py:197
  55.2 1.9 %collective-permute-start.3 = (bf16[4,12,16,512]{3,2,1,0:T(8,128)(2,1)S(1)}, bf16[4,12,16,512]{3,2,1,0:T(8,128)(2,1)}, u32[]{:S(2)}, u32[]{:S(2)}) collective-permute-start(bf16[4,12,16,512]{3,2,1,0:T(8,128)(2,1)S(1)} %all-to-all-done.1.part0), channel_id=1, source_target_pairs={{168,0},{169,1},{170,2},{171,3},{172,4},{173,5},{174,6},{175,7},{1... | collective-permute-start | bytes 2359304 | tf_op jit(solution)/shard_map/ppermute | solution.py:206
  57.1 3.9 %collective-permute-start.1 = (bf16[4,12,16,512]{3,2,1,0:T(8,128)(2,1)S(1)}, bf16[4,12,16,512]{3,2,1,0:T(8,128)(2,1)}, u32[]{:S(2)}, u32[]{:S(2)}) collective-permute-start(bf16[4,12,16,512]{3,2,1,0:T(8,128)(2,1)S(1)} %all-to-all-done.1.part0), channel_id=1, source_target_pairs={{24,0},{25,1},{26,2},{27,3},{28,4},{29,5},{30,6},{31,7},{32,8},{33... | collective-permute-start | bytes 2359304 | tf_op jit(solution)/shard_map/ppermute | solution.py:205
  61.1 5.8 %collective-permute-start.2 = (bf16[4,12,16,512]{3,2,1,0:T(8,128)(2,1)S(1)}, bf16[4,12,16,512]{3,2,1,0:T(8,128)(2,1)}, u32[]{:S(2)}, u32[]{:S(2)}) collective-permute-start(bf16[4,12,16,512]{3,2,1,0:T(8,128)(2,1)S(1)} %all-to-all-done.1.part0), channel_id=1, source_target_pairs={{192,0},{193,1},{194,2},{195,3},{196,4},{197,5},{198,6},{199,7},{2... | collective-permute-start | bytes 2359304 | tf_op jit(solution)/shard_map/ppermute | solution.py:207
  66.9 0.1 pad_add_fusion.at_ref
  67.0 0.0 collective-permute-done.5.left_far_ref
  67.0 0.0 collective-permute-done.4.right_far_ref
  67.0 2.2 %collective-permute-done.3.part3 = bf16[4,12,16,512]{3,2,1,0:T(8,128)(2,1)} collective-permute-done((bf16[4,12,16,512]{3,2,1,0:T(8,128)(2,1)S(1)}, bf16[4,12,16,512]{3,2,1,0:T(8,128)(2,1)}, u32[]{:S(2)}, u32[]{:S(2)}) %collective-permute-start.3) | collective-permute-done | bytes 786464 | tf_op jit(solution)/shard_map/ppermute | solution.py:206
  69.2 0.0 copy-done.3
  69.2 0.0 copy-start.2
  69.2 1.2 %copy-done.2 = bf16[512,1024]{1,0:T(8,128)(2,1)S(1)} copy-done((bf16[512,1024]{1,0:T(8,128)(2,1)S(1)}, bf16[512,1024]{1,0:T(8,128)(2,1)}, u32[]{:S(2)}) %copy-start.2) | copy-done | bytes 1048600
  70.4 3.2 %shard_map.56 = (bf16[128,16,512]{2,1,0:T(8,128)(2,1)S(1)}, bf16[4,512,512]{2,1,0:T(8,128)(2,1)S(1)}, bf16[512,1024]{1,0:T(8,128)(2,1)S(1)}, bf16[512,1024]{1,0:T(8,128)(2,1)S(1)}) custom-call(s32[4]{0:T(128)S(1)} %bitcast.15, s32[4]{0:T(128)S(1)} %collective-permute-done.wanted_far_ref, s32[3]{0:T(128)S(1)} %pad_add_fusion.at_ref, ...), custom_call_target="tpu_custom_call" | custom-call | flops 1073741824 | bytes 8388608 | tf_op jit(solution)/shard_map/pallas_call | solution.py:223
  73.6 0.0 collective-permute-done.1.part1
  73.6 3.4 %collective-permute-done.2.part2 = bf16[4,12,16,512]{3,2,1,0:T(8,128)(2,1)} collective-permute-done((bf16[4,12,16,512]{3,2,1,0:T(8,128)(2,1)S(1)}, bf16[4,12,16,512]{3,2,1,0:T(8,128)(2,1)}, u32[]{:S(2)}, u32[]{:S(2)}) %collective-permute-start.2) | collective-permute-done | bytes 786464 | tf_op jit(solution)/shard_map/ppermute | solution.py:207
  77.1 3.2 %shard_map.57 = (bf16[128,16,512]{2,1,0:T(8,128)(2,1)S(1)}, f32[32,8,512]{2,1,0:T(8,128)S(1)}, bf16[32,8,512]{2,1,0:T(8,128)(2,1)S(1)}) custom-call(s32[4]{0:T(128)S(1)} %bitcast.16, s32[4]{0:T(128)S(1)} %collective-permute-done.wanted_far_ref, s32[3]{0:T(128)S(1)} %pad_add_fusion.at_ref, ...), custom_call_target="tpu_custom_call", output_to_operand_aliasing={{0}: (9, {})} | custom-call | flops 1073741824 | bytes 8388608 | tf_op jit(solution)/shard_map/pallas_call | solution.py:236
  80.3 1.9 %collective-permute-start.6 = (bf16[32,8,512]{2,1,0:T(8,128)(2,1)S(1)}, bf16[32,8,512]{2,1,0:T(8,128)(2,1)S(1)}, u32[]{:S(2)}, u32[]{:S(2)}) collective-permute-start(bf16[32,8,512]{2,1,0:T(8,128)(2,1)S(1)} %get-tuple-element.28), channel_id=1, source_target_pairs={{0,12},{12,0},{1,13},{13,1},{2,14},{14,2},{3,15},{15,3},{4,16},{16... | collective-permute-start | bytes 786440 | tf_op jit(solution)/shard_map/ppermute | solution.py:248
  82.2 1.5 %collective-permute-done.6 = bf16[32,8,512]{2,1,0:T(8,128)(2,1)S(1)} collective-permute-done((bf16[32,8,512]{2,1,0:T(8,128)(2,1)S(1)}, bf16[32,8,512]{2,1,0:T(8,128)(2,1)S(1)}, u32[]{:S(2)}, u32[]{:S(2)}) %collective-permute-start.6) | collective-permute-done | bytes 262176 | tf_op jit(solution)/shard_map/ppermute | solution.py:248
  83.7 0.1 add_convert_fusion
  83.8 22.1 %all_to_all.15 = bf16[32,8,512]{2,1,0:T(8,128)(2,1)S(1)} all-to-all(bf16[32,8,512]{2,1,0:T(8,128)(2,1)S(1)} %add_convert_fusion), channel_id=1, replica_groups=mesh['x'=4,'y'=8,'c'=2,'z'=12] {'x','y'}, dimensions={0} | all-to-all | bytes 524288 | tf_op jit(solution)/shard_map/all_to_all | solution.py:249
  105.9 0.6 reduce_sum.14
  (2 shorter events, 0.0 us)
Async XLA Ops:
  2.1 36.5 %all-to-all-start = ((bf16[24,8,512]{2,1,0:T(8,128)(2,1)}), bf16[24,8,512]{2,1,0:T(8,128)(2,1)S(1)}, u32[]{:S(2)}, u32[]{:S(2)}) async-start(bf16[24,8,512]{2,1,0:T(8,128)(2,1)} %and_select_fusion), calls=%async_computation | async-start | bytes 393216 | tf_op jit(solution)/shard_map/all_to_all | solution.py:185
  21.1 6.8 %collective-permute-start = (s32[4]{0:T(128)}, s32[4]{0:T(128)S(1)}, u32[]{:S(2)}, u32[]{:S(2)}) collective-permute-start(s32[4]{0:T(128)} %bitcast.14), channel_id=1, source_target_pairs={{0,12},{12,0},{1,13},{13,1},{2,14},{14,2},{3,15},{15,3},{4,16},{16... | collective-permute-start | bytes 56 | tf_op jit(solution)/shard_map/ppermute | solution.py:183
  23.0 1.6 %copy-start.4 = (bf16[4,1,512,512]{3,2,1,0:T(8,128)(2,1)S(1)}, bf16[4,1,512,512]{3,2,1,0:T(8,128)(2,1)}, u32[]{:S(2)}) copy-start(bf16[4,1,512,512]{3,2,1,0:T(8,128)(2,1)} %param.7) | copy-start | bytes 6291460
  25.9 1.0 copy-start.1
  26.9 1.0 copy-start.5
  27.9 16.1 %copy-start = (bf16[4,1,512,512]{3,2,1,0:T(8,128)(2,1)S(1)}, bf16[4,1,512,512]{3,2,1,0:T(8,128)(2,1)}, u32[]{:S(2)}) copy-start(bf16[4,1,512,512]{3,2,1,0:T(8,128)(2,1)} %param.8) | copy-start | bytes 6291460
  27.9 41.3 %copy-start.3 = (s32[4,1]{0,1:T(1,128)S(1)}, s32[4,1]{0,1:T(1,128)}, u32[]{:S(2)}) copy-start(s32[4,1]{0,1:T(1,128)} %param.9) | copy-start | bytes 52
  39.7 15.5 %all-to-all-start.1 = ((bf16[4,12,16,512]{3,2,1,0:T(8,128)(2,1)}), bf16[4,12,16,512]{3,2,1,0:T(8,128)(2,1)S(1)}, u32[]{:S(2)}, u32[]{:S(2)}) async-start(bf16[4,12,16,512]{3,2,1,0:T(8,128)(2,1)} %broadcast_in_dim.21), calls=%async_computation.1 | async-start | bytes 1572864 | tf_op jit(solution)/shard_map/all_to_all | solution.py:197
  44.0 23.0 %collective-permute-start.4 = (bf16[4,512,512]{2,1,0:T(8,128)(2,1)S(1)}, bf16[4,512,512]{2,1,0:T(8,128)(2,1)}, u32[]{:S(2)}, u32[]{:S(2)}) collective-permute-start(bf16[4,512,512]{2,1,0:T(8,128)(2,1)S(1)} %bitcast.11), channel_id=1, source_target_pairs={{0,12},{12,0},{1,13},{13,1},{2,14},{14,2},{3,15},{15,3},{4,16},{16... | collective-permute-start | bytes 6291464 | tf_op jit(solution)/shard_map/ppermute | solution.py:182
  45.9 21.1 %collective-permute-start.5 = (bf16[512,1024]{1,0:T(8,128)(2,1)}, bf16[512,1024]{1,0:T(8,128)(2,1)}, u32[]{:S(2)}, u32[]{:S(2)}) collective-permute-start(bf16[512,1024]{1,0:T(8,128)(2,1)} %copy-done.5), channel_id=1, source_target_pairs={{0,12},{12,0},{1,13},{13,1},{2,14},{14,2},{3,15},{15,3},{4,16},{16... | collective-permute-start | bytes 3145736 | tf_op jit(solution)/shard_map/ppermute | solution.py:196
  55.2 14.0 %collective-permute-start.3 = (bf16[4,12,16,512]{3,2,1,0:T(8,128)(2,1)S(1)}, bf16[4,12,16,512]{3,2,1,0:T(8,128)(2,1)}, u32[]{:S(2)}, u32[]{:S(2)}) collective-permute-start(bf16[4,12,16,512]{3,2,1,0:T(8,128)(2,1)S(1)} %all-to-all-done.1.part0), channel_id=1, source_target_pairs={{168,0},{169,1},{170,2},{171,3},{172,4},{173,5},{174,6},{175,7},{1... | collective-permute-start | bytes 2359304 | tf_op jit(solution)/shard_map/ppermute | solution.py:206
  57.1 16.5 %collective-permute-start.1 = (bf16[4,12,16,512]{3,2,1,0:T(8,128)(2,1)S(1)}, bf16[4,12,16,512]{3,2,1,0:T(8,128)(2,1)}, u32[]{:S(2)}, u32[]{:S(2)}) collective-permute-start(bf16[4,12,16,512]{3,2,1,0:T(8,128)(2,1)S(1)} %all-to-all-done.1.part0), channel_id=1, source_target_pairs={{24,0},{25,1},{26,2},{27,3},{28,4},{29,5},{30,6},{31,7},{32,8},{33... | collective-permute-start | bytes 2359304 | tf_op jit(solution)/shard_map/ppermute | solution.py:205
  61.1 16.0 %collective-permute-start.2 = (bf16[4,12,16,512]{3,2,1,0:T(8,128)(2,1)S(1)}, bf16[4,12,16,512]{3,2,1,0:T(8,128)(2,1)}, u32[]{:S(2)}, u32[]{:S(2)}) collective-permute-start(bf16[4,12,16,512]{3,2,1,0:T(8,128)(2,1)S(1)} %all-to-all-done.1.part0), channel_id=1, source_target_pairs={{192,0},{193,1},{194,2},{195,3},{196,4},{197,5},{198,6},{199,7},{2... | collective-permute-start | bytes 2359304 | tf_op jit(solution)/shard_map/ppermute | solution.py:207
  69.2 1.2 %copy-start.2 = (bf16[512,1024]{1,0:T(8,128)(2,1)S(1)}, bf16[512,1024]{1,0:T(8,128)(2,1)}, u32[]{:S(2)}) copy-start(bf16[512,1024]{1,0:T(8,128)(2,1)} %copy-done.1) | copy-start | bytes 3145732
  80.3 3.4 %collective-permute-start.6 = (bf16[32,8,512]{2,1,0:T(8,128)(2,1)S(1)}, bf16[32,8,512]{2,1,0:T(8,128)(2,1)S(1)}, u32[]{:S(2)}, u32[]{:S(2)}) collective-permute-start(bf16[32,8,512]{2,1,0:T(8,128)(2,1)S(1)} %get-tuple-element.28), channel_id=1, source_target_pairs={{0,12},{12,0},{1,13},{13,1},{2,14},{14,2},{3,15},{15,3},{4,16},{16... | collective-permute-start | bytes 786440 | tf_op jit(solution)/shard_map/ppermute | solution.py:248

commit v5 on v4

--- a/solution.py
+++ b/solution.py
@@ -110,11 +110,23 @@
     fetches[2].wait()
 
 
+def middle_products(
+    wanted_ref, wanted_far_ref, at_ref, part1, right_ref, right_far_ref, early_ref, product_ref
+):
+    terms = right_ref.shape[0]
+    for k in range(terms):
+        for sector, right, slot in (
+            (wanted_ref[k], right_ref[k], k),
+            (wanted_far_ref[k], right_far_ref[k], terms + k),
+        ):
+            start = at_ref[0] + 16 - sector
+            multiply((1,), (part1,), sector, start, right, product_ref, slot)
+
+
 def late_sum(
     wanted_ref,
     wanted_far_ref,
     at_ref,
-    part1,
     part2,
     right_ref,
     right_far_ref,
@@ -132,7 +144,7 @@
             (wanted_far_ref[k], right_far_ref[k], terms + k),
         ):
             start = at_ref[0] + 16 - sector
-            multiply((1, 2), (part1, part2), sector, start, right, product_ref, slot)
+            multiply((2,), (part2,), sector, start, right, product_ref, slot)
     middle = terms * HALF // UNIT
     total = jnp.dot(
         left_ref[...],
@@ -233,18 +245,26 @@
         scratch_shapes=[pltpu.SemaphoreType.DMA((3,))],
         **settings,
     )(wanted, wanted_far, at, part, down, right, right_far, left_own, left_far)
+    middle = pl.pallas_call(
+        middle_products,
+        in_specs=[in_smem] * 3 + [in_vmem] * 4,
+        out_specs=in_vmem,
+        out_shape=product_shape,
+        input_output_aliases={6: 0},
+        **settings,
+    )(wanted, wanted_far, at, up, right, right_far, early)
     _, keep, send = pl.pallas_call(
         late_sum,
-        in_specs=[in_smem] * 3 + [in_vmem] * 7,
+        in_specs=[in_smem] * 3 + [in_vmem] * 6,
         out_specs=[in_vmem] * 3,
         out_shape=[
             product_shape,
             jax.ShapeDtypeStruct((NX * NY, ROWS, B), jnp.float32),
             jax.ShapeDtypeStruct((NX * NY, ROWS, B), jnp.bfloat16),
         ],
-        input_output_aliases={9: 0},
+        input_output_aliases={8: 0},
         **settings,
-    )(wanted, wanted_far, at, up, across, right, right_far, left_own, left_far, early)
+    )(wanted, wanted_far, at, across, right, right_far, left_own, left_far, middle)
     chip_sum = keep + lax.ppermute(send, "c", swap).astype(jnp.float32)
     shares = lax.all_to_all(chip_sum.astype(jnp.bfloat16), CHIP, 0, 0, tiled=True)
     return jnp.sum(shares[:, :, None, :].astype(jnp.float32), axis=0).astype(jnp.bfloat16)

time: 107 us -> 107 us (level)
  waiting for transfers between devices: 24.8 us -> 22.8 us
  Pallas kernels: 7.7 us -> 9.59 us
    ppermute x1, waiting for transfers between devices: 3.43 us -> 1.44 us  [on_device(): across = lax.ppermute(part, ALL, shifts((1, 0, 0), (-1, 0, 0)))]
    pallas_call x1 -> x2, Pallas kernels: 3.22 us -> 5.1 us  [the longest x1 3.12 us: on_device(): pl.pallas_call(late_sum, in_specs=[in_smem] * 3 + [in_vmem] * 6, out_spec...]
  transfers between devices with their start and end apart: 9 -> 9, of which waited for: 5 -> 5; matrix products, arithmetic and copies ran while one was open for 0% -> 0% of each run, Pallas kernels for 4% -> 6%
where the time goes in v5:
time: 107 us; the launch traced here: 106 us
  starting transfers between devices  43.1 us (40%)
  waiting for transfers between devices  22.8 us (21%)
  blocking collectives  22.1 us (21%)
  Pallas kernels  9.59 us (9%)
  local copies, waits for them, and re-layouts  5.8 us (5%)
  other arithmetic  2.28 us (2%)
    all_to_all x1, blocking collectives, on_device(): lax.all_to_all(chip_sum.astype(jnp.bfloat16), CHIP, 0, 0, tiled=True)  22.1 us
    all_to_all x1, starting transfers between devices, on_device(): lax.all_to_all(masked, ('y', 'z'), 0, 0, axis_index_groups=far_groups(),...  18.9 us
    all_to_all x1, waiting for transfers between devices, on_device(): lax.all_to_all(masked, ('y', 'z'), 0, 0, axis_index_groups=far_groups(),...  10.8 us
    all_to_all x1, waiting for transfers between devices, on_device(): lax.all_to_all(jnp.broadcast_to(far[None], (NX, NZ, UNIT, B)), ('x', 'y',...  6.89 us
    ppermute x1, starting transfers between devices, on_device(): across = lax.ppermute(part, ALL, shifts((1, 0, 0), (-1, 0, 0)))  5.83 us
    unnamed x12, local copies, waits for them, and re-layouts  4.78 us
    all_to_all x1, starting transfers between devices, on_device(): lax.all_to_all(jnp.broadcast_to(far[None], (NX, NZ, UNIT, B)), ('x', 'y',...  4.29 us
    ppermute x1, starting transfers between devices, on_device(): up = lax.ppermute(part, ALL, shifts((0, 1, 0), (0, 0, 1)))  3.93 us
  transfers between devices with their start and end apart: 9, of which 5 were waited for; matrix products, arithmetic and copies ran while one was open for 0% of the time, Pallas kernels for 6%

profile of v5, /device:TPU:8, one launch (start us, length us, event | category | flops | bytes accessed | tf_op | source)
XLA Modules:
  0.0 106.4 jit_solution(7480737553763331537)
XLA Ops:
  0.7 1.5 %and_select_fusion = bf16[24,8,512]{2,1,0:T(8,128)(2,1)} fusion(pred[512]{0:T(512)(128)(4,1)S(1)} %iota_compare_fusion, pred[8]{0:T(512)(128)(4,1)S(1)} %add_compare_fusion, bf16[8,512]{1,0:T(8,128)(2,1)} %bitcast.21), kind=kLoop, calls=%fused_computation.1 | loop fusion | flops 196608 | bytes 205320 | tf_op jit(solution)/shard_map/jit(_where)/select_n | solution.py:179
  2.1 18.9 %all-to-all-start = ((bf16[24,8,512]{2,1,0:T(8,128)(2,1)}), bf16[24,8,512]{2,1,0:T(8,128)(2,1)S(1)}, u32[]{:S(2)}, u32[]{:S(2)}) async-start(bf16[24,8,512]{2,1,0:T(8,128)(2,1)} %and_select_fusion), calls=%async_computation | async-start | bytes 393216 | tf_op jit(solution)/shard_map/all_to_all | solution.py:197
  21.1 1.9 %collective-permute-start = (s32[4]{0:T(128)}, s32[4]{0:T(128)S(1)}, u32[]{:S(2)}, u32[]{:S(2)}) collective-permute-start(s32[4]{0:T(128)} %bitcast.15), channel_id=1, source_target_pairs={{0,12},{12,0},{1,13},{13,1},{2,14},{14,2},{3,15},{15,3},{4,16},{16... | collective-permute-start | bytes 56 | tf_op jit(solution)/shard_map/ppermute | solution.py:195
  23.0 0.0 copy-start.4
  23.0 1.6 %copy-done.4 = bf16[4,1,512,512]{3,2,1,0:T(8,128)(2,1)S(1)} copy-done((bf16[4,1,512,512]{3,2,1,0:T(8,128)(2,1)S(1)}, bf16[4,1,512,512]{3,2,1,0:T(8,128)(2,1)}, u32[]{:S(2)}) %copy-start.4) | copy-done | bytes 2097176
  24.6 1.3 %shard_map.55 = (bf16[512,1024]{1,0:T(8,128)(2,1)S(1)}, bf16[512,1024]{1,0:T(8,128)(2,1)S(1)}) custom-call(s32[1]{0:T(128)} %bitcast.4.core_ref, bf16[4,512,512]{2,1,0:T(8,128)(2,1)S(1)} %bitcast.19), custom_call_target="tpu_custom_call" | custom-call | flops 1073741824 | bytes 4194304 | tf_op jit(solution)/shard_map/pallas_call | solution.py:186
  25.9 0.0 copy-start.1
  25.9 1.0 copy-done.1
  26.9 0.0 copy-start.5
  26.9 1.0 copy-done.5
  27.9 0.0 copy-start
  27.9 0.0 copy-start.3
  27.9 0.0 collective-permute-done.wanted_far_ref
  27.9 10.8 %all-to-all-done = bf16[24,8,512]{2,1,0:T(8,128)(2,1)S(1)} async-done(((bf16[24,8,512]{2,1,0:T(8,128)(2,1)}), bf16[24,8,512]{2,1,0:T(8,128)(2,1)S(1)}, u32[]{:S(2)}, u32[]{:S(2)}) %all-to-all-start) | async-done | bytes 196640 | tf_op jit(solution)/shard_map/all_to_all | solution.py:197
  38.7 1.0 broadcast_in_dim.21
  39.7 4.3 %all-to-all-start.1 = ((bf16[4,12,16,512]{3,2,1,0:T(8,128)(2,1)}), bf16[4,12,16,512]{3,2,1,0:T(8,128)(2,1)S(1)}, u32[]{:S(2)}, u32[]{:S(2)}) async-start(bf16[4,12,16,512]{3,2,1,0:T(8,128)(2,1)} %broadcast_in_dim.21), calls=%async_computation.1 | async-start | bytes 1572864 | tf_op jit(solution)/shard_map/all_to_all | solution.py:209
  44.0 0.0 copy-done
  44.0 1.9 %collective-permute-start.3 = (bf16[4,512,512]{2,1,0:T(8,128)(2,1)S(1)}, bf16[4,512,512]{2,1,0:T(8,128)(2,1)}, u32[]{:S(2)}, u32[]{:S(2)}) collective-permute-start(bf16[4,512,512]{2,1,0:T(8,128)(2,1)S(1)} %bitcast.11), channel_id=1, source_target_pairs={{0,12},{12,0},{1,13},{13,1},{2,14},{14,2},{3,15},{15,3},{4,16},{16... | collective-permute-start | bytes 6291464 | tf_op jit(solution)/shard_map/ppermute | solution.py:194
  45.9 2.4 %collective-permute-start.4 = (bf16[512,1024]{1,0:T(8,128)(2,1)}, bf16[512,1024]{1,0:T(8,128)(2,1)}, u32[]{:S(2)}, u32[]{:S(2)}) collective-permute-start(bf16[512,1024]{1,0:T(8,128)(2,1)} %copy-done.5), channel_id=1, source_target_pairs={{0,12},{12,0},{1,13},{13,1},{2,14},{14,2},{3,15},{15,3},{4,16},{16... | collective-permute-start | bytes 3145736 | tf_op jit(solution)/shard_map/ppermute | solution.py:208
  48.3 6.9 %all-to-all-done.1.part0 = bf16[4,12,16,512]{3,2,1,0:T(8,128)(2,1)S(1)} async-done(((bf16[4,12,16,512]{3,2,1,0:T(8,128)(2,1)}), bf16[4,12,16,512]{3,2,1,0:T(8,128)(2,1)S(1)}, u32[]{:S(2)}, u32[]{:S(2)}) %all-to-all-start.1) | async-done | bytes 786464 | tf_op jit(solution)/shard_map/all_to_all | solution.py:209
  55.2 1.9 %collective-permute-start.2 = (bf16[4,12,16,512]{3,2,1,0:T(8,128)(2,1)S(1)}, bf16[4,12,16,512]{3,2,1,0:T(8,128)(2,1)}, u32[]{:S(2)}, u32[]{:S(2)}) collective-permute-start(bf16[4,12,16,512]{3,2,1,0:T(8,128)(2,1)S(1)} %all-to-all-done.1.part0), channel_id=1, source_target_pairs={{168,0},{169,1},{170,2},{171,3},{172,4},{173,5},{174,6},{175,7},{1... | collective-permute-start | bytes 2359304 | tf_op jit(solution)/shard_map/ppermute | solution.py:218
  57.1 3.9 %collective-permute-start.5 = (bf16[4,12,16,512]{3,2,1,0:T(8,128)(2,1)S(1)}, bf16[4,12,16,512]{3,2,1,0:T(8,128)(2,1)}, u32[]{:S(2)}, u32[]{:S(2)}) collective-permute-start(bf16[4,12,16,512]{3,2,1,0:T(8,128)(2,1)S(1)} %all-to-all-done.1.part0), channel_id=1, source_target_pairs={{24,0},{25,1},{26,2},{27,3},{28,4},{29,5},{30,6},{31,7},{32,8},{33... | collective-permute-start | bytes 2359304 | tf_op jit(solution)/shard_map/ppermute | solution.py:217
  61.1 5.8 %collective-permute-start.1 = (bf16[4,12,16,512]{3,2,1,0:T(8,128)(2,1)S(1)}, bf16[4,12,16,512]{3,2,1,0:T(8,128)(2,1)}, u32[]{:S(2)}, u32[]{:S(2)}) collective-permute-start(bf16[4,12,16,512]{3,2,1,0:T(8,128)(2,1)S(1)} %all-to-all-done.1.part0), channel_id=1, source_target_pairs={{192,0},{193,1},{194,2},{195,3},{196,4},{197,5},{198,6},{199,7},{2... | collective-permute-start | bytes 2359304 | tf_op jit(solution)/shard_map/ppermute | solution.py:219
  66.9 0.1 pad_add_fusion.at_ref
  67.0 0.0 collective-permute-done.4.left_far_ref
  67.0 0.0 collective-permute-done.3.right_far_ref
  67.0 2.2 %collective-permute-done.2.part3 = bf16[4,12,16,512]{3,2,1,0:T(8,128)(2,1)} collective-permute-done((bf16[4,12,16,512]{3,2,1,0:T(8,128)(2,1)S(1)}, bf16[4,12,16,512]{3,2,1,0:T(8,128)(2,1)}, u32[]{:S(2)}, u32[]{:S(2)}) %collective-permute-start.2) | collective-permute-done | bytes 786464 | tf_op jit(solution)/shard_map/ppermute | solution.py:218
  69.2 0.0 copy-done.3
  69.2 0.0 copy-start.2
  69.2 1.2 %copy-done.2 = bf16[512,1024]{1,0:T(8,128)(2,1)S(1)} copy-done((bf16[512,1024]{1,0:T(8,128)(2,1)S(1)}, bf16[512,1024]{1,0:T(8,128)(2,1)}, u32[]{:S(2)}) %copy-start.2) | copy-done | bytes 1048600
  70.4 3.2 %shard_map.56 = (bf16[128,16,512]{2,1,0:T(8,128)(2,1)S(1)}, bf16[4,512,512]{2,1,0:T(8,128)(2,1)S(1)}, bf16[512,1024]{1,0:T(8,128)(2,1)S(1)}, bf16[512,1024]{1,0:T(8,128)(2,1)S(1)}) custom-call(s32[4]{0:T(128)S(1)} %bitcast.16, s32[4]{0:T(128)S(1)} %collective-permute-done.wanted_far_ref, s32[3]{0:T(128)S(1)} %pad_add_fusion.at_ref, ...), custom_call_target="tpu_custom_call" | custom-call | flops 1073741824 | bytes 8388608 | tf_op jit(solution)/shard_map/pallas_call | solution.py:235
  73.6 0.0 collective-permute-done.5.part1
  73.6 2.0 %shard_map.57.early_ref = bf16[128,16,512]{2,1,0:T(8,128)(2,1)S(1)} custom-call(s32[4]{0:T(128)S(1)} %bitcast.17, s32[4]{0:T(128)S(1)} %collective-permute-done.wanted_far_ref, s32[3]{0:T(128)S(1)} %pad_add_fusion.at_ref, bf16[4,12,16,512]{3,2,1,0:T(8,128)(2,1)} %collective-permute-done.5.part1, ...), custom_call_target="tpu_custom_call", output_to_operand_aliasing={{}: (6, {})} | custom-call | flops 1073741824 | bytes 8388608 | tf_op jit(solution)/shard_map/pallas_call | solution.py:248
  75.6 1.4 %collective-permute-done.1.part2 = bf16[4,12,16,512]{3,2,1,0:T(8,128)(2,1)} collective-permute-done((bf16[4,12,16,512]{3,2,1,0:T(8,128)(2,1)S(1)}, bf16[4,12,16,512]{3,2,1,0:T(8,128)(2,1)}, u32[]{:S(2)}, u32[]{:S(2)}) %collective-permute-start.1) | collective-permute-done | bytes 786464 | tf_op jit(solution)/shard_map/ppermute | solution.py:219
  77.1 3.1 %shard_map.58 = (bf16[128,16,512]{2,1,0:T(8,128)(2,1)S(1)}, f32[32,8,512]{2,1,0:T(8,128)S(1)}, bf16[32,8,512]{2,1,0:T(8,128)(2,1)S(1)}) custom-call(s32[4]{0:T(128)S(1)} %bitcast.18, s32[4]{0:T(128)S(1)} %collective-permute-done.wanted_far_ref, s32[3]{0:T(128)S(1)} %pad_add_fusion.at_ref, ...), custom_call_target="tpu_custom_call", output_to_operand_aliasing={{0}: (8, {})} | custom-call | flops 1073741824 | bytes 8388608 | tf_op jit(solution)/shard_map/pallas_call | solution.py:256
  80.2 1.9 %collective-permute-start.6 = (bf16[32,8,512]{2,1,0:T(8,128)(2,1)S(1)}, bf16[32,8,512]{2,1,0:T(8,128)(2,1)S(1)}, u32[]{:S(2)}, u32[]{:S(2)}) collective-permute-start(bf16[32,8,512]{2,1,0:T(8,128)(2,1)S(1)} %get-tuple-element.28), channel_id=1, source_target_pairs={{0,12},{12,0},{1,13},{13,1},{2,14},{14,2},{3,15},{15,3},{4,16},{16... | collective-permute-start | bytes 786440 | tf_op jit(solution)/shard_map/ppermute | solution.py:268
  82.1 1.5 %collective-permute-done.6 = bf16[32,8,512]{2,1,0:T(8,128)(2,1)S(1)} collective-permute-done((bf16[32,8,512]{2,1,0:T(8,128)(2,1)S(1)}, bf16[32,8,512]{2,1,0:T(8,128)(2,1)S(1)}, u32[]{:S(2)}, u32[]{:S(2)}) %collective-permute-start.6) | collective-permute-done | bytes 262176 | tf_op jit(solution)/shard_map/ppermute | solution.py:268
  83.6 0.1 add_convert_fusion
  83.7 22.1 %all_to_all.15 = bf16[32,8,512]{2,1,0:T(8,128)(2,1)S(1)} all-to-all(bf16[32,8,512]{2,1,0:T(8,128)(2,1)S(1)} %add_convert_fusion), channel_id=1, replica_groups=mesh['x'=4,'y'=8,'c'=2,'z'=12] {'x','y'}, dimensions={0} | all-to-all | bytes 524288 | tf_op jit(solution)/shard_map/all_to_all | solution.py:269
  105.8 0.6 reduce_sum.14
  (2 shorter events, 0.0 us)
Async XLA Ops:
  2.1 36.5 %all-to-all-start = ((bf16[24,8,512]{2,1,0:T(8,128)(2,1)}), bf16[24,8,512]{2,1,0:T(8,128)(2,1)S(1)}, u32[]{:S(2)}, u32[]{:S(2)}) async-start(bf16[24,8,512]{2,1,0:T(8,128)(2,1)} %and_select_fusion), calls=%async_computation | async-start | bytes 393216 | tf_op jit(solution)/shard_map/all_to_all | solution.py:197
  21.1 6.8 %collective-permute-start = (s32[4]{0:T(128)}, s32[4]{0:T(128)S(1)}, u32[]{:S(2)}, u32[]{:S(2)}) collective-permute-start(s32[4]{0:T(128)} %bitcast.15), channel_id=1, source_target_pairs={{0,12},{12,0},{1,13},{13,1},{2,14},{14,2},{3,15},{15,3},{4,16},{16... | collective-permute-start | bytes 56 | tf_op jit(solution)/shard_map/ppermute | solution.py:195
  23.0 1.6 %copy-start.4 = (bf16[4,1,512,512]{3,2,1,0:T(8,128)(2,1)S(1)}, bf16[4,1,512,512]{3,2,1,0:T(8,128)(2,1)}, u32[]{:S(2)}) copy-start(bf16[4,1,512,512]{3,2,1,0:T(8,128)(2,1)} %param.7) | copy-start | bytes 6291460
  25.9 1.0 copy-start.1
  26.9 1.0 copy-start.5
  27.9 16.1 %copy-start = (bf16[4,1,512,512]{3,2,1,0:T(8,128)(2,1)S(1)}, bf16[4,1,512,512]{3,2,1,0:T(8,128)(2,1)}, u32[]{:S(2)}) copy-start(bf16[4,1,512,512]{3,2,1,0:T(8,128)(2,1)} %param.8) | copy-start | bytes 6291460
  27.9 41.3 %copy-start.3 = (s32[4,1]{0,1:T(1,128)S(1)}, s32[4,1]{0,1:T(1,128)}, u32[]{:S(2)}) copy-start(s32[4,1]{0,1:T(1,128)} %param.9) | copy-start | bytes 52
  39.7 15.5 %all-to-all-start.1 = ((bf16[4,12,16,512]{3,2,1,0:T(8,128)(2,1)}), bf16[4,12,16,512]{3,2,1,0:T(8,128)(2,1)S(1)}, u32[]{:S(2)}, u32[]{:S(2)}) async-start(bf16[4,12,16,512]{3,2,1,0:T(8,128)(2,1)} %broadcast_in_dim.21), calls=%async_computation.1 | async-start | bytes 1572864 | tf_op jit(solution)/shard_map/all_to_all | solution.py:209
  44.0 23.0 %collective-permute-start.3 = (bf16[4,512,512]{2,1,0:T(8,128)(2,1)S(1)}, bf16[4,512,512]{2,1,0:T(8,128)(2,1)}, u32[]{:S(2)}, u32[]{:S(2)}) collective-permute-start(bf16[4,512,512]{2,1,0:T(8,128)(2,1)S(1)} %bitcast.11), channel_id=1, source_target_pairs={{0,12},{12,0},{1,13},{13,1},{2,14},{14,2},{3,15},{15,3},{4,16},{16... | collective-permute-start | bytes 6291464 | tf_op jit(solution)/shard_map/ppermute | solution.py:194
  45.9 21.1 %collective-permute-start.4 = (bf16[512,1024]{1,0:T(8,128)(2,1)}, bf16[512,1024]{1,0:T(8,128)(2,1)}, u32[]{:S(2)}, u32[]{:S(2)}) collective-permute-start(bf16[512,1024]{1,0:T(8,128)(2,1)} %copy-done.5), channel_id=1, source_target_pairs={{0,12},{12,0},{1,13},{13,1},{2,14},{14,2},{3,15},{15,3},{4,16},{16... | collective-permute-start | bytes 3145736 | tf_op jit(solution)/shard_map/ppermute | solution.py:208
  55.2 14.0 %collective-permute-start.2 = (bf16[4,12,16,512]{3,2,1,0:T(8,128)(2,1)S(1)}, bf16[4,12,16,512]{3,2,1,0:T(8,128)(2,1)}, u32[]{:S(2)}, u32[]{:S(2)}) collective-permute-start(bf16[4,12,16,512]{3,2,1,0:T(8,128)(2,1)S(1)} %all-to-all-done.1.part0), channel_id=1, source_target_pairs={{168,0},{169,1},{170,2},{171,3},{172,4},{173,5},{174,6},{175,7},{1... | collective-permute-start | bytes 2359304 | tf_op jit(solution)/shard_map/ppermute | solution.py:218
  57.1 16.5 %collective-permute-start.5 = (bf16[4,12,16,512]{3,2,1,0:T(8,128)(2,1)S(1)}, bf16[4,12,16,512]{3,2,1,0:T(8,128)(2,1)}, u32[]{:S(2)}, u32[]{:S(2)}) collective-permute-start(bf16[4,12,16,512]{3,2,1,0:T(8,128)(2,1)S(1)} %all-to-all-done.1.part0), channel_id=1, source_target_pairs={{24,0},{25,1},{26,2},{27,3},{28,4},{29,5},{30,6},{31,7},{32,8},{33... | collective-permute-start | bytes 2359304 | tf_op jit(solution)/shard_map/ppermute | solution.py:217
  61.1 16.0 %collective-permute-start.1 = (bf16[4,12,16,512]{3,2,1,0:T(8,128)(2,1)S(1)}, bf16[4,12,16,512]{3,2,1,0:T(8,128)(2,1)}, u32[]{:S(2)}, u32[]{:S(2)}) collective-permute-start(bf16[4,12,16,512]{3,2,1,0:T(8,128)(2,1)S(1)} %all-to-all-done.1.part0), channel_id=1, source_target_pairs={{192,0},{193,1},{194,2},{195,3},{196,4},{197,5},{198,6},{199,7},{2... | collective-permute-start | bytes 2359304 | tf_op jit(solution)/shard_map/ppermute | solution.py:219
  69.2 1.2 %copy-start.2 = (bf16[512,1024]{1,0:T(8,128)(2,1)S(1)}, bf16[512,1024]{1,0:T(8,128)(2,1)}, u32[]{:S(2)}) copy-start(bf16[512,1024]{1,0:T(8,128)(2,1)} %copy-done.1) | copy-start | bytes 3145732
  80.2 3.4 %collective-permute-start.6 = (bf16[32,8,512]{2,1,0:T(8,128)(2,1)S(1)}, bf16[32,8,512]{2,1,0:T(8,128)(2,1)S(1)}, u32[]{:S(2)}, u32[]{:S(2)}) collective-permute-start(bf16[32,8,512]{2,1,0:T(8,128)(2,1)S(1)} %get-tuple-element.28), channel_id=1, source_target_pairs={{0,12},{12,0},{1,13},{13,1},{2,14},{14,2},{3,15},{15,3},{4,16},{16... | collective-permute-start | bytes 786440 | tf_op jit(solution)/shard_map/ppermute | solution.py:268

commit v6 on v4

--- a/solution.py
+++ b/solution.py
@@ -13,7 +13,7 @@
 ROWS = 8
 HALF = B // 2
 UNIT = 2 * ROWS
-CHIP = ("x", "y")
+CHIP = ("y", "x")
 ALL = ("x", "y", "c", "z")
 
 
@@ -146,7 +146,7 @@
     row = lax.broadcasted_iota(jnp.int32, (B, B), 0)
     col = lax.broadcasted_iota(jnp.int32, (B, B), 1)
     total = jnp.where((row < at_ref[2]) & (col < at_ref[2]), total, 0.0)
-    pairs = total.reshape(NX * NY, 2, ROWS, B)
+    pairs = jnp.swapaxes(total.reshape(NX, NY, 2, ROWS, B), 0, 1).reshape(NX * NY, 2, ROWS, B)
     low, high = pairs[:, 0], pairs[:, 1]
     first = at_ref[1] == 0
     keep_ref[...] = jnp.where(first, low, high)

time: 107 us -> 107 us (level)
  no operation moved by 1% of the time
where the time goes in v6:
time: 107 us; the launch traced here: 106 us
  starting transfers between devices  43.1 us (40%)
  waiting for transfers between devices  24.8 us (23%)
  blocking collectives  22 us (21%)
  Pallas kernels  7.7 us (7%)
  local copies, waits for them, and re-layouts  5.8 us (5%)
  other arithmetic  2.28 us (2%)
    all_to_all x1, blocking collectives, on_device(): lax.all_to_all(chip_sum.astype(jnp.bfloat16), CHIP, 0, 0, tiled=True)  22 us
    all_to_all x1, starting transfers between devices, on_device(): lax.all_to_all(masked, ('y', 'z'), 0, 0, axis_index_groups=far_groups(),...  18.9 us
    all_to_all x1, waiting for transfers between devices, on_device(): lax.all_to_all(masked, ('y', 'z'), 0, 0, axis_index_groups=far_groups(),...  10.8 us
    all_to_all x1, waiting for transfers between devices, on_device(): lax.all_to_all(jnp.broadcast_to(far[None], (NX, NZ, UNIT, B)), ('x', 'y',...  6.89 us
    ppermute x1, starting transfers between devices, on_device(): across = lax.ppermute(part, ALL, shifts((1, 0, 0), (-1, 0, 0)))  5.83 us
    unnamed x12, local copies, waits for them, and re-layouts  4.78 us
    all_to_all x1, starting transfers between devices, on_device(): lax.all_to_all(jnp.broadcast_to(far[None], (NX, NZ, UNIT, B)), ('x', 'y',...  4.29 us
    ppermute x1, starting transfers between devices, on_device(): up = lax.ppermute(part, ALL, shifts((0, 1, 0), (0, 0, 1)))  3.93 us
  transfers between devices with their start and end apart: 9, of which 5 were waited for; matrix products, arithmetic and copies ran while one was open for 0% of the time, Pallas kernels for 4%

profile of v6, /device:TPU:8, one launch (start us, length us, event | category | flops | bytes accessed | tf_op | source)
XLA Modules:
  0.0 106.4 jit_solution(9516823424896477877)
XLA Ops:
  0.7 1.5 %and_select_fusion = bf16[24,8,512]{2,1,0:T(8,128)(2,1)} fusion(pred[512]{0:T(512)(128)(4,1)S(1)} %iota_compare_fusion, pred[8]{0:T(512)(128)(4,1)S(1)} %add_compare_fusion, bf16[8,512]{1,0:T(8,128)(2,1)} %bitcast.19), kind=kLoop, calls=%fused_computation.1 | loop fusion | flops 196608 | bytes 205320 | tf_op jit(solution)/shard_map/jit(_where)/select_n | solution.py:167
  2.1 18.9 %all-to-all-start = ((bf16[24,8,512]{2,1,0:T(8,128)(2,1)}), bf16[24,8,512]{2,1,0:T(8,128)(2,1)S(1)}, u32[]{:S(2)}, u32[]{:S(2)}) async-start(bf16[24,8,512]{2,1,0:T(8,128)(2,1)} %and_select_fusion), calls=%async_computation | async-start | bytes 393216 | tf_op jit(solution)/shard_map/all_to_all | solution.py:185
  21.1 1.9 %collective-permute-start = (s32[4]{0:T(128)}, s32[4]{0:T(128)S(1)}, u32[]{:S(2)}, u32[]{:S(2)}) collective-permute-start(s32[4]{0:T(128)} %bitcast.14), channel_id=1, source_target_pairs={{0,12},{12,0},{1,13},{13,1},{2,14},{14,2},{3,15},{15,3},{4,16},{16... | collective-permute-start | bytes 56 | tf_op jit(solution)/shard_map/ppermute | solution.py:183
  23.0 0.0 copy-start.4
  23.0 1.6 %copy-done.4 = bf16[4,1,512,512]{3,2,1,0:T(8,128)(2,1)S(1)} copy-done((bf16[4,1,512,512]{3,2,1,0:T(8,128)(2,1)S(1)}, bf16[4,1,512,512]{3,2,1,0:T(8,128)(2,1)}, u32[]{:S(2)}) %copy-start.4) | copy-done | bytes 2097176
  24.6 1.3 %shard_map.55 = (bf16[512,1024]{1,0:T(8,128)(2,1)S(1)}, bf16[512,1024]{1,0:T(8,128)(2,1)S(1)}) custom-call(s32[1]{0:T(128)} %bitcast.4.core_ref, bf16[4,512,512]{2,1,0:T(8,128)(2,1)S(1)} %bitcast.17), custom_call_target="tpu_custom_call" | custom-call | flops 1073741824 | bytes 4194304 | tf_op jit(solution)/shard_map/pallas_call | solution.py:174
  25.9 0.0 copy-start.1
  25.9 1.0 copy-done.1
  26.9 0.0 copy-start.5
  26.9 1.0 copy-done.5
  27.9 0.0 copy-start
  27.9 0.0 copy-start.3
  27.9 0.0 collective-permute-done.wanted_far_ref
  27.9 10.8 %all-to-all-done = bf16[24,8,512]{2,1,0:T(8,128)(2,1)S(1)} async-done(((bf16[24,8,512]{2,1,0:T(8,128)(2,1)}), bf16[24,8,512]{2,1,0:T(8,128)(2,1)S(1)}, u32[]{:S(2)}, u32[]{:S(2)}) %all-to-all-start) | async-done | bytes 196640 | tf_op jit(solution)/shard_map/all_to_all | solution.py:185
  38.7 1.0 broadcast_in_dim.21
  39.7 4.3 %all-to-all-start.1 = ((bf16[4,12,16,512]{3,2,1,0:T(8,128)(2,1)}), bf16[4,12,16,512]{3,2,1,0:T(8,128)(2,1)S(1)}, u32[]{:S(2)}, u32[]{:S(2)}) async-start(bf16[4,12,16,512]{3,2,1,0:T(8,128)(2,1)} %broadcast_in_dim.21), calls=%async_computation.1 | async-start | bytes 1572864 | tf_op jit(solution)/shard_map/all_to_all | solution.py:197
  44.0 0.0 copy-done
  44.0 1.9 %collective-permute-start.4 = (bf16[4,512,512]{2,1,0:T(8,128)(2,1)S(1)}, bf16[4,512,512]{2,1,0:T(8,128)(2,1)}, u32[]{:S(2)}, u32[]{:S(2)}) collective-permute-start(bf16[4,512,512]{2,1,0:T(8,128)(2,1)S(1)} %bitcast.11), channel_id=1, source_target_pairs={{0,12},{12,0},{1,13},{13,1},{2,14},{14,2},{3,15},{15,3},{4,16},{16... | collective-permute-start | bytes 6291464 | tf_op jit(solution)/shard_map/ppermute | solution.py:182
  45.9 2.4 %collective-permute-start.5 = (bf16[512,1024]{1,0:T(8,128)(2,1)}, bf16[512,1024]{1,0:T(8,128)(2,1)}, u32[]{:S(2)}, u32[]{:S(2)}) collective-permute-start(bf16[512,1024]{1,0:T(8,128)(2,1)} %copy-done.5), channel_id=1, source_target_pairs={{0,12},{12,0},{1,13},{13,1},{2,14},{14,2},{3,15},{15,3},{4,16},{16... | collective-permute-start | bytes 3145736 | tf_op jit(solution)/shard_map/ppermute | solution.py:196
  48.3 6.9 %all-to-all-done.1.part0 = bf16[4,12,16,512]{3,2,1,0:T(8,128)(2,1)S(1)} async-done(((bf16[4,12,16,512]{3,2,1,0:T(8,128)(2,1)}), bf16[4,12,16,512]{3,2,1,0:T(8,128)(2,1)S(1)}, u32[]{:S(2)}, u32[]{:S(2)}) %all-to-all-start.1) | async-done | bytes 786464 | tf_op jit(solution)/shard_map/all_to_all | solution.py:197
  55.2 1.9 %collective-permute-start.3 = (bf16[4,12,16,512]{3,2,1,0:T(8,128)(2,1)S(1)}, bf16[4,12,16,512]{3,2,1,0:T(8,128)(2,1)}, u32[]{:S(2)}, u32[]{:S(2)}) collective-permute-start(bf16[4,12,16,512]{3,2,1,0:T(8,128)(2,1)S(1)} %all-to-all-done.1.part0), channel_id=1, source_target_pairs={{168,0},{169,1},{170,2},{171,3},{172,4},{173,5},{174,6},{175,7},{1... | collective-permute-start | bytes 2359304 | tf_op jit(solution)/shard_map/ppermute | solution.py:206
  57.1 3.9 %collective-permute-start.1 = (bf16[4,12,16,512]{3,2,1,0:T(8,128)(2,1)S(1)}, bf16[4,12,16,512]{3,2,1,0:T(8,128)(2,1)}, u32[]{:S(2)}, u32[]{:S(2)}) collective-permute-start(bf16[4,12,16,512]{3,2,1,0:T(8,128)(2,1)S(1)} %all-to-all-done.1.part0), channel_id=1, source_target_pairs={{24,0},{25,1},{26,2},{27,3},{28,4},{29,5},{30,6},{31,7},{32,8},{33... | collective-permute-start | bytes 2359304 | tf_op jit(solution)/shard_map/ppermute | solution.py:205
  61.1 5.8 %collective-permute-start.2 = (bf16[4,12,16,512]{3,2,1,0:T(8,128)(2,1)S(1)}, bf16[4,12,16,512]{3,2,1,0:T(8,128)(2,1)}, u32[]{:S(2)}, u32[]{:S(2)}) collective-permute-start(bf16[4,12,16,512]{3,2,1,0:T(8,128)(2,1)S(1)} %all-to-all-done.1.part0), channel_id=1, source_target_pairs={{192,0},{193,1},{194,2},{195,3},{196,4},{197,5},{198,6},{199,7},{2... | collective-permute-start | bytes 2359304 | tf_op jit(solution)/shard_map/ppermute | solution.py:207
  66.9 0.1 pad_add_fusion.at_ref
  67.0 0.0 collective-permute-done.5.left_far_ref
  67.0 0.0 collective-permute-done.4.right_far_ref
  67.0 2.2 %collective-permute-done.3.part3 = bf16[4,12,16,512]{3,2,1,0:T(8,128)(2,1)} collective-permute-done((bf16[4,12,16,512]{3,2,1,0:T(8,128)(2,1)S(1)}, bf16[4,12,16,512]{3,2,1,0:T(8,128)(2,1)}, u32[]{:S(2)}, u32[]{:S(2)}) %collective-permute-start.3) | collective-permute-done | bytes 786464 | tf_op jit(solution)/shard_map/ppermute | solution.py:206
  69.2 0.0 copy-done.3
  69.2 0.0 copy-start.2
  69.2 1.2 %copy-done.2 = bf16[512,1024]{1,0:T(8,128)(2,1)S(1)} copy-done((bf16[512,1024]{1,0:T(8,128)(2,1)S(1)}, bf16[512,1024]{1,0:T(8,128)(2,1)}, u32[]{:S(2)}) %copy-start.2) | copy-done | bytes 1048600
  70.4 3.2 %shard_map.56 = (bf16[128,16,512]{2,1,0:T(8,128)(2,1)S(1)}, bf16[4,512,512]{2,1,0:T(8,128)(2,1)S(1)}, bf16[512,1024]{1,0:T(8,128)(2,1)S(1)}, bf16[512,1024]{1,0:T(8,128)(2,1)S(1)}) custom-call(s32[4]{0:T(128)S(1)} %bitcast.15, s32[4]{0:T(128)S(1)} %collective-permute-done.wanted_far_ref, s32[3]{0:T(128)S(1)} %pad_add_fusion.at_ref, ...), custom_call_target="tpu_custom_call" | custom-call | flops 1073741824 | bytes 8388608 | tf_op jit(solution)/shard_map/pallas_call | solution.py:223
  73.6 0.0 collective-permute-done.1.part1
  73.6 3.4 %collective-permute-done.2.part2 = bf16[4,12,16,512]{3,2,1,0:T(8,128)(2,1)} collective-permute-done((bf16[4,12,16,512]{3,2,1,0:T(8,128)(2,1)S(1)}, bf16[4,12,16,512]{3,2,1,0:T(8,128)(2,1)}, u32[]{:S(2)}, u32[]{:S(2)}) %collective-permute-start.2) | collective-permute-done | bytes 786464 | tf_op jit(solution)/shard_map/ppermute | solution.py:207
  77.1 3.2 %shard_map.57 = (bf16[128,16,512]{2,1,0:T(8,128)(2,1)S(1)}, f32[32,8,512]{2,1,0:T(8,128)S(1)}, bf16[32,8,512]{2,1,0:T(8,128)(2,1)S(1)}) custom-call(s32[4]{0:T(128)S(1)} %bitcast.16, s32[4]{0:T(128)S(1)} %collective-permute-done.wanted_far_ref, s32[3]{0:T(128)S(1)} %pad_add_fusion.at_ref, ...), custom_call_target="tpu_custom_call", output_to_operand_aliasing={{0}: (9, {})} | custom-call | flops 1073741824 | bytes 8388608 | tf_op jit(solution)/shard_map/pallas_call | solution.py:236
  80.3 1.9 %collective-permute-start.6 = (bf16[32,8,512]{2,1,0:T(8,128)(2,1)S(1)}, bf16[32,8,512]{2,1,0:T(8,128)(2,1)S(1)}, u32[]{:S(2)}, u32[]{:S(2)}) collective-permute-start(bf16[32,8,512]{2,1,0:T(8,128)(2,1)S(1)} %get-tuple-element.28), channel_id=1, source_target_pairs={{0,12},{12,0},{1,13},{13,1},{2,14},{14,2},{3,15},{15,3},{4,16},{16... | collective-permute-start | bytes 786440 | tf_op jit(solution)/shard_map/ppermute | solution.py:248
  82.2 1.5 %collective-permute-done.6 = bf16[32,8,512]{2,1,0:T(8,128)(2,1)S(1)} collective-permute-done((bf16[32,8,512]{2,1,0:T(8,128)(2,1)S(1)}, bf16[32,8,512]{2,1,0:T(8,128)(2,1)S(1)}, u32[]{:S(2)}, u32[]{:S(2)}) %collective-permute-start.6) | collective-permute-done | bytes 262176 | tf_op jit(solution)/shard_map/ppermute | solution.py:248
  83.7 0.1 add_convert_fusion
  83.8 22.0 %all_to_all.15 = bf16[32,8,512]{2,1,0:T(8,128)(2,1)S(1)} all-to-all(bf16[32,8,512]{2,1,0:T(8,128)(2,1)S(1)} %add_convert_fusion), channel_id=1, replica_groups=mesh['x'=4,'y'=8,'c'=2,'z'=12] {'y','x'}, dimensions={0} | all-to-all | bytes 524288 | tf_op jit(solution)/shard_map/all_to_all | solution.py:249
  105.8 0.6 reduce_sum.14
  (2 shorter events, 0.0 us)
Async XLA Ops:
  2.1 36.5 %all-to-all-start = ((bf16[24,8,512]{2,1,0:T(8,128)(2,1)}), bf16[24,8,512]{2,1,0:T(8,128)(2,1)S(1)}, u32[]{:S(2)}, u32[]{:S(2)}) async-start(bf16[24,8,512]{2,1,0:T(8,128)(2,1)} %and_select_fusion), calls=%async_computation | async-start | bytes 393216 | tf_op jit(solution)/shard_map/all_to_all | solution.py:185
  21.1 6.8 %collective-permute-start = (s32[4]{0:T(128)}, s32[4]{0:T(128)S(1)}, u32[]{:S(2)}, u32[]{:S(2)}) collective-permute-start(s32[4]{0:T(128)} %bitcast.14), channel_id=1, source_target_pairs={{0,12},{12,0},{1,13},{13,1},{2,14},{14,2},{3,15},{15,3},{4,16},{16... | collective-permute-start | bytes 56 | tf_op jit(solution)/shard_map/ppermute | solution.py:183
  23.0 1.6 %copy-start.4 = (bf16[4,1,512,512]{3,2,1,0:T(8,128)(2,1)S(1)}, bf16[4,1,512,512]{3,2,1,0:T(8,128)(2,1)}, u32[]{:S(2)}) copy-start(bf16[4,1,512,512]{3,2,1,0:T(8,128)(2,1)} %param.7) | copy-start | bytes 6291460
  25.9 1.0 copy-start.1
  26.9 1.0 copy-start.5
  27.9 16.1 %copy-start = (bf16[4,1,512,512]{3,2,1,0:T(8,128)(2,1)S(1)}, bf16[4,1,512,512]{3,2,1,0:T(8,128)(2,1)}, u32[]{:S(2)}) copy-start(bf16[4,1,512,512]{3,2,1,0:T(8,128)(2,1)} %param.8) | copy-start | bytes 6291460
  27.9 41.3 %copy-start.3 = (s32[4,1]{0,1:T(1,128)S(1)}, s32[4,1]{0,1:T(1,128)}, u32[]{:S(2)}) copy-start(s32[4,1]{0,1:T(1,128)} %param.9) | copy-start | bytes 52
  39.7 15.5 %all-to-all-start.1 = ((bf16[4,12,16,512]{3,2,1,0:T(8,128)(2,1)}), bf16[4,12,16,512]{3,2,1,0:T(8,128)(2,1)S(1)}, u32[]{:S(2)}, u32[]{:S(2)}) async-start(bf16[4,12,16,512]{3,2,1,0:T(8,128)(2,1)} %broadcast_in_dim.21), calls=%async_computation.1 | async-start | bytes 1572864 | tf_op jit(solution)/shard_map/all_to_all | solution.py:197
  44.0 23.0 %collective-permute-start.4 = (bf16[4,512,512]{2,1,0:T(8,128)(2,1)S(1)}, bf16[4,512,512]{2,1,0:T(8,128)(2,1)}, u32[]{:S(2)}, u32[]{:S(2)}) collective-permute-start(bf16[4,512,512]{2,1,0:T(8,128)(2,1)S(1)} %bitcast.11), channel_id=1, source_target_pairs={{0,12},{12,0},{1,13},{13,1},{2,14},{14,2},{3,15},{15,3},{4,16},{16... | collective-permute-start | bytes 6291464 | tf_op jit(solution)/shard_map/ppermute | solution.py:182
  45.9 21.1 %collective-permute-start.5 = (bf16[512,1024]{1,0:T(8,128)(2,1)}, bf16[512,1024]{1,0:T(8,128)(2,1)}, u32[]{:S(2)}, u32[]{:S(2)}) collective-permute-start(bf16[512,1024]{1,0:T(8,128)(2,1)} %copy-done.5), channel_id=1, source_target_pairs={{0,12},{12,0},{1,13},{13,1},{2,14},{14,2},{3,15},{15,3},{4,16},{16... | collective-permute-start | bytes 3145736 | tf_op jit(solution)/shard_map/ppermute | solution.py:196
  55.2 14.0 %collective-permute-start.3 = (bf16[4,12,16,512]{3,2,1,0:T(8,128)(2,1)S(1)}, bf16[4,12,16,512]{3,2,1,0:T(8,128)(2,1)}, u32[]{:S(2)}, u32[]{:S(2)}) collective-permute-start(bf16[4,12,16,512]{3,2,1,0:T(8,128)(2,1)S(1)} %all-to-all-done.1.part0), channel_id=1, source_target_pairs={{168,0},{169,1},{170,2},{171,3},{172,4},{173,5},{174,6},{175,7},{1... | collective-permute-start | bytes 2359304 | tf_op jit(solution)/shard_map/ppermute | solution.py:206
  57.1 16.5 %collective-permute-start.1 = (bf16[4,12,16,512]{3,2,1,0:T(8,128)(2,1)S(1)}, bf16[4,12,16,512]{3,2,1,0:T(8,128)(2,1)}, u32[]{:S(2)}, u32[]{:S(2)}) collective-permute-start(bf16[4,12,16,512]{3,2,1,0:T(8,128)(2,1)S(1)} %all-to-all-done.1.part0), channel_id=1, source_target_pairs={{24,0},{25,1},{26,2},{27,3},{28,4},{29,5},{30,6},{31,7},{32,8},{33... | collective-permute-start | bytes 2359304 | tf_op jit(solution)/shard_map/ppermute | solution.py:205
  61.1 16.0 %collective-permute-start.2 = (bf16[4,12,16,512]{3,2,1,0:T(8,128)(2,1)S(1)}, bf16[4,12,16,512]{3,2,1,0:T(8,128)(2,1)}, u32[]{:S(2)}, u32[]{:S(2)}) collective-permute-start(bf16[4,12,16,512]{3,2,1,0:T(8,128)(2,1)S(1)} %all-to-all-done.1.part0), channel_id=1, source_target_pairs={{192,0},{193,1},{194,2},{195,3},{196,4},{197,5},{198,6},{199,7},{2... | collective-permute-start | bytes 2359304 | tf_op jit(solution)/shard_map/ppermute | solution.py:207
  69.2 1.2 %copy-start.2 = (bf16[512,1024]{1,0:T(8,128)(2,1)S(1)}, bf16[512,1024]{1,0:T(8,128)(2,1)}, u32[]{:S(2)}) copy-start(bf16[512,1024]{1,0:T(8,128)(2,1)} %copy-done.1) | copy-start | bytes 3145732
  80.3 3.4 %collective-permute-start.6 = (bf16[32,8,512]{2,1,0:T(8,128)(2,1)S(1)}, bf16[32,8,512]{2,1,0:T(8,128)(2,1)S(1)}, u32[]{:S(2)}, u32[]{:S(2)}) collective-permute-start(bf16[32,8,512]{2,1,0:T(8,128)(2,1)S(1)} %get-tuple-element.28), channel_id=1, source_target_pairs={{0,12},{12,0},{1,13},{13,1},{2,14},{14,2},{3,15},{15,3},{4,16},{16... | collective-permute-start | bytes 786440 | tf_op jit(solution)/shard_map/ppermute | solution.py:248
